TPU v7x, 32 devices: a whole 2x2x4 slice. The times are simulated.
32 devices in a mesh: grp: 2 (over y), gx: 16 (over z, x, core).
Axes of the slice: x: 2, y: 2, z: 4, core: 2. Of those that a mesh axis runs over, the one named last changes fastest.
Arguments:
- features: bfloat16 [128, 32, 64, 128], P('grp', 'gx'), parts along dimension 0, may hold values from -6 to 6
- cotangent: bfloat16 [128, 32, 64, 128], P('grp', 'gx'), parts along dimension 0, may hold values from -6 to 6
- spectral_weight: bfloat16 [16384, 64, 128], P('gx'), may hold values from -0.5 to 0.5
- channel_weight: bfloat16 [64, 64], replicated, may hold values from -0.75 to 0.75
- channel_bias: float32 [64], replicated, may hold values from -3 to 3
Outputs:
- activated: bfloat16 [128, 32, 64, 128], P('grp', 'gx'), parts along dimension 0
- feature_grad: bfloat16 [128, 32, 64, 128], P('grp', 'gx'), parts along dimension 0
- spectral_grad: bfloat16 [32768, 64, 128], P(('grp', 'gx')), parts along dimension 0
There are 2 independent parts, one for each index of `grp`. A program takes and returns all parts, laid end to end along the dimension named above; an argument that names none is the same for every part. Nothing has to cross between parts.
All inputs are finite; a program needn't handle non-finite values.
Results may differ from a plain program's by a relative error of at most 0.018.
Values may be sent and summed in bfloat16 or wider, within the bound.
No kernel may reach another device: no remote copies, remote signals or barrier semaphores. Data moves between devices by JAX's collectives and lax.ppermute only.
A program may use at most 192 MiB of HBM per device.

v0:
```python
import functools
import math

import jax
import jax.numpy as jnp
import ml_dtypes
import numpy as np
from jax import lax
from jax.experimental import pallas as pl
from jax.experimental.pallas import tpu as pltpu
from jax.sharding import PartitionSpec as P

MX = 32
MY = 32
MZ = 16


SQRT_TWO_PI = math.sqrt(2.0 / math.pi)
CUBIC_COEF = 0.044715


def freq_index(retained, length):
    ladder = jnp.arange(retained, dtype=jnp.int32)
    return jnp.where(ladder < retained // 2, ladder, length - retained + ladder)


def cos_sin(wavenum, length):
    points = jnp.arange(length, dtype=jnp.int32)
    angles = (wavenum[:, None] * points[None, :] % length).astype(jnp.float32) * (
        2.0 * math.pi / length
    )
    return (jnp.cos(angles), jnp.sin(angles))


def analysis_pair(wavenum, length):
    cosine, sine_wave = cos_sin(wavenum, length)
    cosine, sine_wave = (cosine.T, sine_wave.T)
    return jnp.stack(
        [jnp.stack([cosine, -sine_wave], 1), jnp.stack([sine_wave, cosine], 1)], 1
    ).astype(jnp.bfloat16)


def synthesis_pair(wavenum, length):
    cosine, sine_wave = cos_sin(wavenum, length)
    return jnp.stack(
        [jnp.stack([cosine, sine_wave], 1), jnp.stack([-sine_wave, cosine], 1)], 1
    ).astype(jnp.bfloat16)


def depth_table(retained, length):
    cosine, sine_wave = cos_sin(jnp.arange(retained, dtype=jnp.int32), length)
    return jnp.concatenate([cosine, -sine_wave], 0).astype(jnp.bfloat16)


def gelu_parts(inputs):
    cubed_in = inputs * inputs * inputs
    tangent = jnp.tanh(SQRT_TWO_PI * (inputs + CUBIC_COEF * cubed_in))
    output = 0.5 * inputs * (1.0 + tangent)
    derivative = 0.5 * (1.0 + tangent) + 0.5 * inputs * (1.0 - tangent * tangent) * SQRT_TWO_PI * (
        1.0 + 3.0 * CUBIC_COEF * inputs * inputs
    )
    return (output, derivative)


def mode_product(coeffs, weights, channels):
    stacked = coeffs.reshape(coeffs.shape[0], 2, channels)
    halves = jnp.einsum("mac,mcj->amj", stacked, weights, preferred_element_type=jnp.float32)
    real_out = halves[0, :, :channels] - halves[1, :, channels:]
    imag_out = halves[0, :, channels:] + halves[1, :, :channels]
    return jnp.concatenate([real_out, imag_out], 1).astype(jnp.bfloat16)


def mode_grads(coeffs, weights, grad_modes, channels, weight_scale, input_scale):
    number = coeffs.shape[0]
    stacked = coeffs.reshape(number, 2, channels)
    grad_pairs = grad_modes.reshape(number, 2, channels)
    real_w = jnp.einsum("mac,mao->mco", stacked, grad_pairs, preferred_element_type=jnp.float32)
    imag_w = jnp.einsum(
        "mc,mo->mco", stacked[:, 0], grad_pairs[:, 1], preferred_element_type=jnp.float32
    ) - jnp.einsum(
        "mc,mo->mco", stacked[:, 1], grad_pairs[:, 0], preferred_element_type=jnp.float32
    )
    weight_grad = (jnp.concatenate([real_w, imag_w], 2) * weight_scale).astype(jnp.bfloat16)
    straight = jnp.concatenate([grad_pairs[:, 0], grad_pairs[:, 1]], 1)
    rotated = jnp.concatenate([grad_pairs[:, 1], -grad_pairs[:, 0]], 1)
    real_x = jnp.einsum("mcj,mj->mc", weights, straight, preferred_element_type=jnp.float32)
    imag_x = jnp.einsum("mcj,mj->mc", weights, rotated, preferred_element_type=jnp.float32)
    input_grad = (jnp.concatenate([real_x, imag_x], 1) * input_scale).astype(jnp.bfloat16)
    return (weight_grad, input_grad)


def general_body(features, cotangent, spectral_weight, channel_weight, channel_bias):
    channels, planes, lines, depth_len = features.shape
    devices = lax.axis_size("gx")
    all_planes = planes * devices
    owned_modes = spectral_weight.shape[0]
    wave_pairs = MY * MZ
    forward_scale = 1.0 / math.sqrt(all_planes * lines * depth_len)
    inverse_scale = 1.0 / math.sqrt(MX * wave_pairs)
    weight_scale = math.sqrt(MX * wave_pairs / (all_planes * lines * depth_len))
    depth_basis = depth_table(MZ, depth_len)
    across_y = analysis_pair(freq_index(MY, lines), lines)
    back_y = synthesis_pair(freq_index(MY, lines), lines)
    across_full = analysis_pair(freq_index(MX, all_planes), all_planes)
    back_full = synthesis_pair(freq_index(MX, all_planes), all_planes)
    depth_part = jnp.dot(features, depth_basis.T, preferred_element_type=jnp.float32).astype(
        jnp.bfloat16
    )
    plane_part = (
        jnp.einsum(
            "cxyaz,yabk->cxbkz",
            depth_part.reshape(channels, planes, lines, 2, MZ),
            across_y,
            preferred_element_type=jnp.float32,
        )
        .astype(jnp.bfloat16)
        .reshape(channels, planes, 2, wave_pairs)
    )
    all_rows = lax.all_to_all(plane_part, "gx", split_axis=3, concat_axis=1, tiled=True)
    mode_sums = jnp.einsum(
        "cxaq,xabk->qkbc", all_rows, across_full, preferred_element_type=jnp.float32
    ).reshape(owned_modes, 2 * channels)
    coeffs = (mode_sums * forward_scale).astype(jnp.bfloat16)
    spectral = mode_product(coeffs, spectral_weight, channels)
    planes_all = jnp.einsum(
        "qkao,kabx->oxbq",
        spectral.reshape(owned_modes // MX, MX, 2, channels),
        back_full,
        preferred_element_type=jnp.float32,
    ).astype(jnp.bfloat16)
    planes_back = lax.all_to_all(planes_all, "gx", split_axis=1, concat_axis=3, tiled=True)
    lines_back = (
        jnp.einsum(
            "oxakz,kaby->oxybz",
            planes_back.reshape(channels, planes, 2, MY, MZ),
            back_y,
            preferred_element_type=jnp.float32,
        )
        .astype(jnp.bfloat16)
        .reshape(channels, planes, lines, 2 * MZ)
    )
    spectral_term = (
        jnp.dot(lines_back, depth_basis, preferred_element_type=jnp.float32) * inverse_scale
    )
    pointwise = jnp.einsum(
        "oc,cxyz->oxyz", channel_weight, features, preferred_element_type=jnp.float32
    )
    hidden = spectral_term + pointwise + channel_bias[:, None, None, None]
    activated, derivative = gelu_parts(hidden)
    upstream = (cotangent.astype(jnp.float32) * derivative).astype(jnp.bfloat16)
    lines_grad = (
        jnp.dot(upstream, depth_basis.T, preferred_element_type=jnp.float32) * inverse_scale
    ).astype(jnp.bfloat16)
    rows_grad = (
        jnp.einsum(
            "oxybz,kaby->oxakz",
            lines_grad.reshape(channels, planes, lines, 2, MZ),
            back_y,
            preferred_element_type=jnp.float32,
        )
        .astype(jnp.bfloat16)
        .reshape(channels, planes, 2, wave_pairs)
    )
    all_grads = lax.all_to_all(rows_grad, "gx", split_axis=3, concat_axis=1, tiled=True)
    grad_sums = jnp.einsum(
        "oxbq,kabx->qkao", all_grads, back_full, preferred_element_type=jnp.float32
    ).reshape(owned_modes, 2 * channels)
    grad_modes = grad_sums.astype(jnp.bfloat16)
    spectral_grad, coeff_grad = mode_grads(
        coeffs, spectral_weight, grad_modes, channels, weight_scale, forward_scale
    )
    plane_all = jnp.einsum(
        "qkbc,xabk->cxaq",
        coeff_grad.reshape(owned_modes // MX, MX, 2, channels),
        across_full,
        preferred_element_type=jnp.float32,
    ).astype(jnp.bfloat16)
    plane_grad = lax.all_to_all(plane_all, "gx", split_axis=1, concat_axis=3, tiled=True)
    depth_grad = (
        jnp.einsum(
            "cxbkz,yabk->cxyaz",
            plane_grad.reshape(channels, planes, 2, MY, MZ),
            across_y,
            preferred_element_type=jnp.float32,
        )
        .astype(jnp.bfloat16)
        .reshape(channels, planes, lines, 2 * MZ)
    )
    channel_back = jnp.einsum(
        "oc,oxyz->cxyz", channel_weight, upstream, preferred_element_type=jnp.float32
    )
    feature_grad = (
        jnp.dot(depth_grad, depth_basis, preferred_element_type=jnp.float32) + channel_back
    ).astype(jnp.bfloat16)
    return (activated.astype(jnp.bfloat16), feature_grad, spectral_grad)


PLANES = 2
GROUP = 8
STEP = 16
VMEM_MIB = 32
VECTOR = 2
WAITS = {0: 4, 4: 4, 8: 4, 12: 2, 14: 1, 15: 1}
NT = (((1,), (1,)), ((), ()))
F32 = jnp.float32
BF16 = jnp.bfloat16


def np_freq(retained, length):
    ladder = np.arange(retained)
    return np.where(ladder < retained // 2, ladder, length - retained + ladder)


def np_angles(wavenum, length):
    points = np.arange(length)
    return (wavenum[:, None] * points[None, :] % length) * (2.0 * math.pi / length)


def as_bf16(table):
    return np.asarray(table, np.float32).astype(ml_dtypes.bfloat16)


def rotation(angle, sign):
    cosine, sine_wave = np.cos(angle), sign * np.sin(angle)
    return np.stack([np.stack([cosine, -sine_wave]), np.stack([sine_wave, cosine])])


@functools.lru_cache(maxsize=None)
def tables(devices, lines, depth_len):
    planes_all = devices * PLANES
    angle = np_angles(np.arange(MZ), depth_len)
    depth = np.stack([np.cos(angle), -np.sin(angle)])
    eye = np.eye(GROUP)
    depth_block = np.einsum("akz,ij->akijz", depth, eye).reshape(2 * MZ * GROUP, GROUP * depth_len)
    depth_pair = np.einsum("akz,ij->iakjz", depth, np.eye(2)).reshape(4 * MZ, 2 * depth_len)
    plane_eye = np.eye(PLANES)
    angle = np_angles(np_freq(MY, lines), lines).reshape(devices, MY // devices, lines)
    across = np.einsum("badly,xw->ldbxawy", rotation(angle, -1.0), plane_eye)
    across = across.reshape(MY * 2 * PLANES, 2 * PLANES * lines)
    back = np.einsum("pbdly,xw->pxyldbw", rotation(angle, 1.0), plane_eye)
    back = back.reshape(2 * PLANES * lines, MY * 2 * PLANES)
    angle = np_angles(np_freq(MX, planes_all), planes_all).reshape(MX // 4, 4, devices, PLANES)
    forward = rotation(angle, -1.0)
    rows = np.einsum("batksx->tbksax", forward).reshape(MX // 4, 2, 4, devices * 2 * PLANES)
    plain = rows.reshape(2 * MX, -1)
    both = np.stack([rows, rows[:, ::-1]], 1).reshape(4 * MX, -1)
    turned = np.concatenate([rows[:, 1:], -rows[:, :1]], 1).reshape(2 * MX, -1)
    straight_rotated = np.concatenate([plain, turned], 0)
    inverse = np.einsum("batksx->sbxtak", rotation(angle, 1.0)).reshape(-1, 2 * MX)
    return {
        "depth": as_bf16(depth_block),
        "depth_pair": as_bf16(depth_pair),
        "across_y": as_bf16(across),
        "back_y": as_bf16(back),
        "plain_x": as_bf16(plain),
        "both_x": as_bf16(both),
        "straight_x": as_bf16(straight_rotated),
        "back_x": as_bf16(inverse),
    }


def dot_nn(left, right):
    return jnp.dot(left, right, preferred_element_type=F32)


def dot_nt(left, right):
    return lax.dot_general(left, right, NT, preferred_element_type=F32)


def lanes(shape):
    return lax.broadcasted_iota(jnp.int32, shape, len(shape) - 1)


def sublanes(shape):
    return lax.broadcasted_iota(jnp.int32, shape, len(shape) - 2)


def swap_halves(block):
    return pltpu.roll(block, 64, 1)


def part_copy(source, target, sems, index, size):
    start = index * size if isinstance(index, int) else pl.multiple_of(index * size, size)
    part = pl.ds(start, size)
    return pltpu.make_async_copy(source.at[part], target.at[part], sems.at[index])


def start_parts(source, target, sems, size):
    for index in range(source.shape[0] // size):
        part_copy(source, target, sems, index, size).start()


def start_tables(pairs, sems):
    copies = []
    for index, (source, target) in enumerate(pairs):
        copy = pltpu.make_async_copy(source, target, sems.at[index])
        copy.start()
        copies.append(copy)
    return copies


def depth_quad(slabs, quad, depth_pair, scale, group, lines_ref):
    four = slabs[quad * 4 : quad * 4 + 4]
    wide = jnp.concatenate(
        [jnp.concatenate(four[2 * pair : 2 * pair + 2], axis=1) for pair in range(2)], axis=0
    )
    parts = dot_nt(depth_pair, wide)
    if scale is not None:
        parts = parts * scale
    half = wide.shape[0] // 2
    for pair in range(2):
        start = (group * GROUP + quad * 4 + pair * 2) * 2 * MZ
        if not isinstance(start, int):
            start = pl.multiple_of(start, 4 * MZ)
        lines_ref[pl.ds(start, 4 * MZ), :] = parts[:, pair * half : (pair + 1) * half]


def depth_analysis(slabs, depth_pair, scale, group, lines_ref):
    for quad in range(2):
        depth_quad(slabs, quad, depth_pair, scale, group, lines_ref)


def rows_analysis(lines_ref, across_ref, rows_ref, out_ref):
    channels = lines_ref.shape[0] // (2 * MZ)
    across = across_ref[...]
    half = across.shape[0] // 2
    for kzh in range(MZ // 2):
        pair = jnp.concatenate(
            [
                jnp.concatenate(
                    [
                        lines_ref[pl.ds(a * MZ + 2 * kzh + h, channels, stride=2 * MZ), :]
                        for a in range(2)
                    ],
                    axis=1,
                )
                for h in range(2)
            ],
            axis=0,
        ).astype(BF16)
        rows = dot_nt(across, pair)
        for kyl in range(2):
            rows_ref[pl.ds(kyl * 8 + kzh, half, stride=16), :] = rows[
                kyl * half : (kyl + 1) * half
            ]
    out_ref[...] = rows_ref[...].astype(BF16)


def rows_gather(block_ref, rows_ref, spec_ref):
    rows_ref[...] = block_ref[...].astype(F32)
    count = rows_ref.shape[0] // 16
    eye = (sublanes((128, 128)) == lanes((128, 128))).astype(BF16)
    for kzh in range(MZ // 2):
        both = jnp.concatenate(
            [rows_ref[pl.ds(kyl * 8 + kzh, count, stride=16), :] for kyl in range(2)], axis=0
        ).astype(BF16)
        turned = dot_nt(eye, both)
        for h in range(2):
            spec_ref[:, (2 * kzh + h) * GROUP : (2 * kzh + h + 1) * GROUP, :] = turned[
                h * 64 : (h + 1) * 64
            ].reshape(8, GROUP, turned.shape[1])


def lines_synthesis(step, spec_ref, back, scale):
    count = STEP // GROUP
    both = jnp.concatenate([spec_ref[step * count + g] for g in range(count)], axis=0)
    lines = dot_nt(back, both.astype(BF16))
    if scale is not None:
        lines = lines * scale
    lines = lines.astype(BF16)
    half = lines.shape[0] // 2
    return [
        jnp.concatenate(
            [lines[p * half : (p + 1) * half, g * 128 : (g + 1) * 128] for p in range(2)], axis=1
        )
        for g in range(count)
    ]


def flat(slab):
    return slab.reshape(slab.shape[0] * slab.shape[1], slab.shape[2])


def analysis_kernel(
    field_hbm,
    pair_hbm,
    across_hbm,
    out_ref,
    field_ref,
    pair_ref,
    across_ref,
    lines_ref,
    rows_ref,
    field_sems,
    table_sems,
):
    first, second = start_tables([(pair_hbm, pair_ref), (across_hbm, across_ref)], table_sems)
    start_parts(field_hbm, field_ref, field_sems, STEP)
    first.wait()

    @pl.loop(0, field_ref.shape[0] // STEP)
    def _(step):
        part_copy(field_hbm, field_ref, field_sems, step, STEP).wait()
        for g in range(STEP // GROUP):
            group = step * (STEP // GROUP) + g
            slabs = [flat(field_ref[group * GROUP + ci]) for ci in range(GROUP)]
            depth_analysis(slabs, pair_ref[...], None, group, lines_ref)

    second.wait()
    rows_analysis(lines_ref, across_ref, rows_ref, out_ref)


def middle_kernel(
    inverse_scale,
    block_ref,
    bias_ref,
    point_hbm,
    cot_hbm,
    depth_hbm,
    pair_hbm,
    across_hbm,
    back_hbm,
    act_hbm,
    up_hbm,
    out_ref,
    point_ref,
    cot_ref,
    depth_ref,
    pair_ref,
    across_ref,
    back_ref,
    act_ref,
    up_ref,
    lines_ref,
    rows_ref,
    spec_ref,
    point_sems,
    cot_sems,
    act_sems,
    up_sems,
    table_sems,
):
    tables_in = start_tables(
        [
            (back_hbm, back_ref),
            (depth_hbm, depth_ref),
            (pair_hbm, pair_ref),
            (across_hbm, across_ref),
        ],
        table_sems,
    )
    start_parts(point_hbm, point_ref, point_sems, STEP)
    start_parts(cot_hbm, cot_ref, cot_sems, STEP)
    rows_gather(block_ref, rows_ref, spec_ref)
    for copy in tables_in:
        copy.wait()
    steps = point_ref.shape[0] // STEP
    groups = point_ref.shape[0] // GROUP
    per_step = STEP // GROUP

    def activate(index, spectral):
        hidden = spectral + flat(point_ref[index]).astype(F32) + bias_ref[index]
        square = hidden * hidden
        gate = 0.5 + 0.5 * jnp.tanh(hidden * (SQRT_TWO_PI + (SQRT_TWO_PI * CUBIC_COEF) * square))
        slope = hidden * (2.0 * SQRT_TWO_PI + (6.0 * SQRT_TWO_PI * CUBIC_COEF) * square)
        derivative = gate + (gate - gate * gate) * slope
        upstream = (flat(cot_ref[index]).astype(F32) * derivative).astype(BF16)
        act_ref[index] = (hidden * gate).astype(BF16).reshape(act_ref.shape[1:])
        up_ref[index] = upstream.reshape(up_ref.shape[1:])
        return upstream

    def quarter(wide, at):
        return dot_nn(wide, depth_ref[:, at * 256 : (at + 1) * 256])

    wides = lines_synthesis(0, spec_ref, back_ref[...], inverse_scale)
    spectral = [quarter(wides[0], at) for at in range(4)]
    last = None
    for group in range(groups):
        step = group // per_step
        if group % per_step == 0:
            part_copy(point_hbm, point_ref, point_sems, step, STEP).wait()
            part_copy(cot_hbm, cot_ref, cot_sems, step, STEP).wait()
            if step + 1 < steps:
                wides += lines_synthesis(step + 1, spec_ref, back_ref[...], inverse_scale)
        following, slabs = [], []
        for at in range(4):
            if group + 1 < groups:
                following.append(quarter(wides[group + 1], at))
            for k in range(2):
                oi = 2 * at + k
                slabs.append(
                    activate(group * GROUP + oi, spectral[at][:, k * 128 : (k + 1) * 128])
                )
            if last is not None and at % 2 == 0:
                depth_quad(last, at // 2, pair_ref[...], inverse_scale, group - 1, lines_ref)
        if group % per_step == per_step - 1:
            part_copy(act_ref, act_hbm, act_sems, step, STEP).start()
            part_copy(up_ref, up_hbm, up_sems, step, STEP).start()
        spectral, last = following, slabs
    depth_analysis(last, pair_ref[...], inverse_scale, groups - 1, lines_ref)
    rows_analysis(lines_ref, across_ref, rows_ref, out_ref)
    for step in range(steps):
        part_copy(act_ref, act_hbm, act_sems, step, STEP).wait()
        part_copy(up_ref, up_hbm, up_sems, step, STEP).wait()


def final_kernel(
    block_ref,
    point_hbm,
    depth_hbm,
    back_hbm,
    out_hbm,
    point_ref,
    depth_ref,
    back_ref,
    out_ref,
    rows_ref,
    spec_ref,
    point_sems,
    out_sems,
    table_sems,
):
    tables_in = start_tables([(back_hbm, back_ref), (depth_hbm, depth_ref)], table_sems)
    start_parts(point_hbm, point_ref, point_sems, STEP)
    rows_gather(block_ref, rows_ref, spec_ref)
    for copy in tables_in:
        copy.wait()
    steps = point_ref.shape[0] // STEP

    @pl.loop(0, steps)
    def _(step):
        part_copy(point_hbm, point_ref, point_sems, step, STEP).wait()
        for g, wide in enumerate(lines_synthesis(step, spec_ref, back_ref[...], None)):
            spectral = dot_nn(wide, depth_ref[...])
            for ci in range(GROUP):
                index = (step * (STEP // GROUP) + g) * GROUP + ci
                total = spectral[:, ci * 128 : (ci + 1) * 128] + flat(point_ref[index]).astype(F32)
                out_ref[index] = total.astype(BF16).reshape(out_ref.shape[1:])
        part_copy(out_ref, out_hbm, out_sems, step, STEP).start()

    for step in range(steps):
        part_copy(out_ref, out_hbm, out_sems, step, STEP).wait()


def point_kernel(
    transposed, weight_ref, field_hbm, out_hbm, field_ref, out_ref, wide_ref, in_sems, out_sems
):
    size = wide_ref.shape[0]
    planes = field_ref.shape[1]
    copies = []
    for plane in range(planes):
        part = (slice(None), pl.ds(plane, 1))
        copy = pltpu.make_async_copy(field_hbm.at[part], field_ref.at[part], in_sems.at[plane])
        copy.start()
        copies.append(copy)
    tall = (sublanes((size, 64)) // 16 == lanes((size, 64))).astype(BF16)
    weight = weight_ref[...]
    left = dot_nt(tall, weight) if transposed else dot_nn(tall, weight)
    left = left.astype(BF16)
    rows = size // 4
    same = sublanes((rows, size)) % 16 == lanes((rows, size)) % 16
    for quarter in range(4):
        spread = dot_nt(left[quarter * rows : (quarter + 1) * rows], tall)
        wide_ref[quarter * rows : (quarter + 1) * rows, :] = jnp.where(same, spread, 0.0).astype(
            BF16
        )
    sends = []
    for plane in range(planes):
        copies[plane].wait()
        for pair in range(2):
            right = jnp.concatenate(
                [
                    field_ref[:, plane, yc * 16 : (yc + 1) * 16, :].reshape(size, 128)
                    for yc in (2 * pair, 2 * pair + 1)
                ],
                axis=1,
            )
            result = dot_nn(wide_ref[...], right).astype(BF16)
            for k in range(2):
                yc = 2 * pair + k
                out_ref[:, plane, yc * 16 : (yc + 1) * 16, :] = result[
                    :, k * 128 : (k + 1) * 128
                ].reshape(size // 16, 16, 128)
        part = (slice(None), pl.ds(plane, 1))
        copy = pltpu.make_async_copy(out_ref.at[part], out_hbm.at[part], out_sems.at[plane])
        copy.start()
        sends.append(copy)
    for copy in sends:
        copy.wait()


def start_weights(weight_hbm, weight_ref, sems):
    copies = []
    for j in range(16):
        rows = weight_ref.shape[0] // 16
        part = pl.ds(j * rows, rows)
        copy = pltpu.make_async_copy(weight_hbm.at[part], weight_ref.at[part], sems.at[j])
        copy.start()
        copies.append(copy)
    return copies


def mode_pair(weight_ref, j, h, u):
    start = ((j * 2 + h) * MX + 8 * u) * 64
    return jnp.concatenate(
        [weight_ref[start : start + 256, :], weight_ref[start + 256 : start + 512, :]], axis=1
    )


def plane_sums(back_ref, mixed_ref, res_ref, quarter):
    count = res_ref.shape[0] // 16
    wide = jnp.concatenate([mixed_ref[quarter * 4 + k] for k in range(4)], axis=1)
    rows = dot_nn(back_ref[...], wide)
    for k in range(4):
        res_ref[pl.ds(quarter * 4 + k, count, stride=16), :] = rows[:, k * 128 : (k + 1) * 128]


def mode_kernel(
    scale,
    block_ref,
    weight_hbm,
    both_ref,
    plain_ref,
    back_ref,
    coeff_hbm,
    out_ref,
    coeff_ref,
    weight_ref,
    rows_ref,
    res_ref,
    left_ref,
    mixed_ref,
    sems,
    coeff_sems,
):
    copies = start_weights(weight_hbm, weight_ref, sems)
    count = rows_ref.shape[0] // 16
    rows_ref[...] = block_ref[...].astype(F32)
    low = lanes((128, 128)) < 64
    kxl = sublanes((128, 128)) % 4
    half = lanes((128, 128)) // 64
    first = (kxl == half).astype(BF16)
    second = (kxl == 2 + half).astype(BF16)
    low8 = lanes((8, 128)) < 64
    sign = jnp.where(sublanes((8, 128)) < 4, -1.0, 1.0)
    for quarter in range(4):
        wide = jnp.concatenate(
            [rows_ref[pl.ds(quarter * 4 + k, count, stride=16), :] for k in range(4)], axis=1
        ).astype(BF16)
        plain = (dot_nn(plain_ref[...], wide) * scale).astype(BF16)
        both = dot_nn(both_ref[...], wide) * scale
        for k in range(4):
            j = quarter * 4 + k
            coeff_ref[j] = plain[:, k * 128 : (k + 1) * 128]
            coeffs = both[:, k * 128 : (k + 1) * 128]
            swapped = swap_halves(coeffs)
            for h in range(2):
                twice = jnp.where(low if h == 0 else ~low, coeffs, swapped).astype(BF16)
                left_ref[j, h] = jnp.concatenate([twice * first, twice * second], axis=1)
    send = pltpu.make_async_copy(coeff_ref, coeff_hbm, coeff_sems.at[0])
    send.start()
    for j in range(16):
        for copy in copies[j : j + WAITS.get(j, 0)]:
            copy.wait()
        mixed = []
        for u in range(MX // 8):
            halves = [
                dot_nn(left_ref[j, h, u * 32 : (u + 1) * 32, :], mode_pair(weight_ref, j, h, u))
                for h in range(2)
            ]
            for t in range(2):
                low_h, high_h = [
                    part[t * 16 : (t + 1) * 16, t * 128 : (t + 1) * 128] for part in halves
                ]
                keep = jnp.where(low8, low_h[:8], sign * high_h[8:])
                move = jnp.where(low8, high_h[:8], sign * low_h[8:])
                mixed.append(keep + swap_halves(move))
        mixed_ref[j] = jnp.concatenate(mixed, axis=0).astype(BF16)
        if j % 4 == 3:
            plane_sums(back_ref, mixed_ref, res_ref, j // 4)
    out_ref[...] = res_ref[...].astype(BF16)
    send.wait()


def mode_grad_kernel(
    scale,
    block_ref,
    weight_hbm,
    straight_ref,
    back_ref,
    coeff_hbm,
    pair_ref,
    coeff_ref,
    out_ref,
    weight_ref,
    rows_ref,
    res_ref,
    mixed_ref,
    sems,
    coeff_sems,
):
    send = pltpu.make_async_copy(coeff_hbm, coeff_ref, coeff_sems.at[0])
    send.start()
    copies = start_weights(weight_hbm, weight_ref, sems)
    count = rows_ref.shape[0] // 16
    rows_ref[...] = block_ref[...].astype(F32)
    low = lanes((64, 128)) < 64
    low16 = lanes((16, 128)) < 64
    row = sublanes((16, 128)) % 4
    upper = row < 2
    valid = lanes((16, 128)) // 64 == row % 2
    even = (sublanes((16, 128)) < 8).astype(BF16)
    odd = (sublanes((16, 128)) >= 8).astype(BF16)
    for j in range(16):
        section = rows_ref[pl.ds(j, count, stride=16), :]
        swapped = swap_halves(section)
        twice = jnp.concatenate(
            [jnp.where(low, section, swapped), jnp.where(low, swapped, section)], axis=1
        ).astype(BF16)
        turned = dot_nn(straight_ref[...], twice)
        for h in range(2):
            part = turned[:, h * 128 : (h + 1) * 128]
            pair_ref[2 * j + h] = jnp.where(low, part[:64], part[64:]).astype(BF16)
    for j in range(16):
        for copy in copies[j : j + WAITS.get(j, 0)]:
            copy.wait()
        mixed = []
        for u in range(MX // 8):
            found = []
            for h in range(2):
                pair = pair_ref[2 * j + h, u * 16 : (u + 1) * 16, :]
                rows = dot_nt(
                    jnp.concatenate([pair * even, pair * odd], axis=1),
                    mode_pair(weight_ref, j, h, u),
                )
                found.append(jnp.where(valid, jnp.where(upper, rows[:, :128], rows[:, 128:]), 0.0))
            keep = jnp.where(low16, found[0], found[1])
            move = jnp.where(low16, found[1], found[0])
            mixed.append(keep + swap_halves(move))
        mixed_ref[j] = (jnp.concatenate(mixed, axis=0) * scale).astype(BF16)
        if j % 4 == 3:
            plane_sums(back_ref, mixed_ref, res_ref, j // 4)
    out_ref[...] = res_ref[...].astype(BF16)
    send.wait()


def weight_grad_kernel(scale, coeff_ref, pair_ref, out_hbm, out_ref, mask_ref, pairs_ref, sems):
    lane = lanes((128, 64))
    part = sublanes((128, 64)) // 64
    for t in range(MX // 4 - VECTOR):
        mask_ref[t] = ((lane // 8 == t) & (lane % 4 // 2 == part)).astype(BF16)
    eye = (sublanes((128, 128)) == lanes((128, 128))).astype(BF16)
    even = (sublanes((64, 128)) % 2 == 0).astype(BF16)
    odd = (sublanes((64, 128)) % 2 == 1).astype(BF16)

    @pl.loop(0, 16)
    def _(j):
        turned = (dot_nt(eye, coeff_ref[j]) * scale).astype(BF16)
        for h in range(2):
            one = turned[h * 64 : (h + 1) * 64]
            left = jnp.concatenate([one, one], axis=0)
            pair = pair_ref[j * 2 + h]
            pairs_ref[h] = pair.astype(F32)
            right = jnp.concatenate([pair * even, pair * odd], axis=1)
            for t in range(MX // 4):
                mode = (j * 2 + h) * MX + 4 * t
                if t < MX // 4 - VECTOR:
                    four = dot_nn(left * mask_ref[t], right)
                    for k in range(4):
                        out_ref[mode + k] = four[
                            k // 2 * 64 : (k // 2 + 1) * 64, k % 2 * 128 : (k % 2 + 1) * 128
                        ].astype(BF16)
                    continue
                for k in range(4):
                    total = None
                    for b in range(2):
                        at = t * 8 + b * 4 + k
                        column = jnp.broadcast_to(one[:, at : at + 1], (64, 128))
                        row = jnp.broadcast_to(pairs_ref[h, at : at + 1, :], (64, 128)).astype(BF16)
                        total = column * row if total is None else total + column * row
                    out_ref[mode + k] = total
        part_copy(out_ref, out_hbm, sems, j, 2 * MX).start()

    for j in range(16):
        part_copy(out_ref, out_hbm, sems, j, 2 * MX).wait()


def params(mib):
    return pltpu.CompilerParams(vmem_limit_bytes=mib * 1024 * 1024)


def cost(flops, moved):
    return pl.CostEstimate(flops=int(flops), bytes_accessed=int(moved), transcendentals=0)


def fast_body(features, cotangent, spectral_weight, channel_weight, channel_bias):
    channels, planes, lines, depth_len = features.shape
    devices = lax.axis_size("gx")
    owned_modes = spectral_weight.shape[0]
    wave_pairs = MY * MZ
    volume = planes * devices * lines * depth_len
    forward_scale = 1.0 / math.sqrt(volume)
    inverse_scale = 1.0 / math.sqrt(MX * wave_pairs)
    weight_scale = math.sqrt(MX * wave_pairs / volume)
    table = {name: jnp.asarray(value) for name, value in tables(devices, lines, depth_len).items()}
    for name in ("depth", "depth_pair", "across_y", "back_y"):
        table[name] = pltpu.with_memory_space_constraint(table[name], pltpu.HBM)
    block_rows = devices * 64
    block_shape = jax.ShapeDtypeStruct((block_rows, 128), BF16)
    vmem = pl.BlockSpec(memory_space=pltpu.VMEM)
    hbm = pl.BlockSpec(memory_space=pltpu.HBM)
    smem = pl.BlockSpec(memory_space=pltpu.SMEM)
    field_scratch = pltpu.VMEM(features.shape, BF16)
    field_shape = jax.ShapeDtypeStruct(features.shape, BF16)

    def sems(count):
        return pltpu.SemaphoreType.DMA((count,))

    def scratch(name):
        return pltpu.VMEM(table[name].shape, BF16)

    def in_hbm(array):
        return pltpu.with_memory_space_constraint(array, pltpu.HBM)

    steps = channels // STEP
    lines_scratch = pltpu.VMEM((channels * 2 * MZ, planes * lines), F32)
    rows_scratch = pltpu.VMEM((block_rows, 128), F32)
    spec_scratch = pltpu.VMEM((channels // GROUP, MZ * GROUP, 128), F32)
    weight_rows = pltpu.with_memory_space_constraint(
        spectral_weight.reshape(owned_modes * channels, 2 * channels), pltpu.HBM
    )
    field_bytes = features.size * 2

    def exchange(block):
        return lax.all_to_all(
            block.reshape(devices, 64, 128), "gx", 0, 0, tiled=True
        ).reshape(block_rows, 128)

    def point(field, transposed):
        return pl.pallas_call(
            functools.partial(point_kernel, transposed),
            out_shape=pltpu.HBM(features.shape, BF16),
            in_specs=[vmem, hbm],
            out_specs=hbm,
            scratch_shapes=[
                field_scratch,
                field_scratch,
                pltpu.VMEM((channels * 16, channels * 16), BF16),
                sems(planes),
                sems(planes),
            ],
            compiler_params=params(VMEM_MIB),
            cost_estimate=cost(2 * 1024**3, 2 * field_bytes),
            name="channel_map_back" if transposed else "channel_map",
        )(channel_weight, in_hbm(field))

    block = pl.pallas_call(
        analysis_kernel,
        out_shape=block_shape,
        in_specs=[hbm, hbm, hbm],
        out_specs=vmem,
        scratch_shapes=[
            field_scratch,
            scratch("depth_pair"),
            scratch("across_y"),
            lines_scratch,
            rows_scratch,
            sems(steps),
            sems(2),
        ],
        compiler_params=params(VMEM_MIB),
        cost_estimate=cost(2 * 256 * 1024 * 1024, field_bytes),
        name="field_analysis",
    )(in_hbm(features), table["depth_pair"], table["across_y"])
    block, pointwise = lax.optimization_barrier((exchange(block), point(features, False)))

    weight_scratch = pltpu.VMEM(weight_rows.shape, BF16)
    mixed_scratch = pltpu.VMEM((16, 64, 128), BF16)
    weight_sems = sems(16)
    coeffs, block = pl.pallas_call(
        functools.partial(mode_kernel, forward_scale),
        out_shape=[pltpu.HBM((16, 64, 128), BF16), block_shape],
        in_specs=[vmem, hbm, vmem, vmem, vmem],
        out_specs=[hbm, vmem],
        scratch_shapes=[
            pltpu.VMEM((16, 64, 128), BF16),
            weight_scratch,
            rows_scratch,
            rows_scratch,
            pltpu.VMEM((16, 2, 128, 256), BF16),
            mixed_scratch,
            weight_sems,
            sems(1),
        ],
        compiler_params=params(VMEM_MIB),
        cost_estimate=cost(256 * 2 * 16 * 256 * 128, 17 * 2**20),
        name="mode_product",
    )(block, weight_rows, table["both_x"], table["plain_x"], table["back_x"])
    block = exchange(block)

    activated, upstream, block = pl.pallas_call(
        functools.partial(middle_kernel, inverse_scale),
        out_shape=[field_shape, pltpu.HBM(features.shape, BF16), block_shape],
        in_specs=[vmem, smem, hbm, hbm, hbm, hbm, hbm, hbm],
        out_specs=[hbm, hbm, vmem],
        scratch_shapes=[
            field_scratch,
            field_scratch,
            scratch("depth"),
            scratch("depth_pair"),
            scratch("across_y"),
            scratch("back_y"),
            field_scratch,
            field_scratch,
            lines_scratch,
            rows_scratch,
            spec_scratch,
            sems(steps),
            sems(steps),
            sems(steps),
            sems(steps),
            sems(4),
        ],
        compiler_params=params(VMEM_MIB),
        cost_estimate=cost(2**30, 4 * field_bytes),
        name="gelu_and_gradient",
    )(
        block,
        channel_bias,
        in_hbm(pointwise),
        in_hbm(cotangent),
        table["depth"],
        table["depth_pair"],
        table["across_y"],
        table["back_y"],
    )
    block = exchange(block)
    block, channel_back = lax.optimization_barrier((block, point(upstream, True)))

    pairs, coeffs, block = pl.pallas_call(
        functools.partial(mode_grad_kernel, forward_scale),
        out_shape=[
            pltpu.VMEM((32, 64, 128), BF16),
            pltpu.VMEM((16, 64, 128), BF16),
            block_shape,
        ],
        in_specs=[vmem, hbm, vmem, vmem, hbm],
        out_specs=[vmem, vmem, vmem],
        scratch_shapes=[
            weight_scratch,
            rows_scratch,
            rows_scratch,
            mixed_scratch,
            weight_sems,
            sems(1),
        ],
        compiler_params=params(VMEM_MIB),
        cost_estimate=cost(256 * 2 * 16 * 256 * 128, 17 * 2**20),
        name="mode_gradient",
    )(block, weight_rows, table["straight_x"], table["back_x"], in_hbm(coeffs))
    block = exchange(block)

    spectral_grad = pl.pallas_call(
        functools.partial(weight_grad_kernel, weight_scale),
        out_shape=jax.ShapeDtypeStruct(spectral_weight.shape, BF16),
        in_specs=[vmem, vmem],
        out_specs=hbm,
        scratch_shapes=[
            pltpu.VMEM(spectral_weight.shape, BF16),
            pltpu.VMEM((MX // 4, 128, 64), BF16),
            pltpu.VMEM((2, 64, 128), F32),
            sems(16),
        ],
        compiler_params=params(VMEM_MIB),
        cost_estimate=cost(512 * 2 * 64 * 64 * 256, 17 * 2**20),
        name="weight_gradient",
    )(
        pltpu.with_memory_space_constraint(coeffs, pltpu.VMEM),
        pltpu.with_memory_space_constraint(pairs, pltpu.VMEM),
    )

    feature_grad = pl.pallas_call(
        final_kernel,
        out_shape=field_shape,
        in_specs=[vmem, hbm, hbm, hbm],
        out_specs=hbm,
        scratch_shapes=[
            field_scratch,
            scratch("depth"),
            scratch("back_y"),
            field_scratch,
            rows_scratch,
            spec_scratch,
            sems(steps),
            sems(steps),
            sems(2),
        ],
        compiler_params=params(VMEM_MIB),
        cost_estimate=cost(2**29, 2 * field_bytes),
        name="field_gradient",
    )(block, in_hbm(channel_back), table["depth"], table["back_y"])
    return (activated, feature_grad, spectral_grad)


def body(features, cotangent, spectral_weight, channel_weight, channel_bias):
    channels, planes, lines, depth_len = features.shape
    devices = lax.axis_size("gx")
    fits = (
        (channels, planes, lines, depth_len) == (64, PLANES, 64, 128)
        and spectral_weight.shape[0] == 2 * MZ * MX
        and devices * 2 == MY
        and devices * 2 == MX
    )
    run = fast_body if fits else general_body
    return run(features, cotangent, spectral_weight, channel_weight, channel_bias)


def solution(mesh):
    in_specs = (
        P("grp", "gx", None, None),
        P("grp", "gx", None, None),
        P("gx", None, None),
        P(),
        P(),
    )
    out_specs = (
        P("grp", "gx", None, None),
        P("grp", "gx", None, None),
        P(("grp", "gx"), None, None),
    )
    return jax.shard_map(body, mesh=mesh, in_specs=in_specs, out_specs=out_specs, check_vma=False)
```

profile of v0, /device:TPU:0, one launch (start us, length us, event | category | flops | bytes accessed | tf_op | source)
XLA Modules:
  0.0 91.7 jit_solution(11378289906620459198)
XLA Ops:
  0.6 0.0 copy-start.5
  0.6 3.8 %field_analysis.1 = bf16[1024,128]{1,0:T(8,128)(2,1)} custom-call(bf16[64,2,64,128]{3,2,1,0:T(8,128)(2,1)} %field_hbm.3, bf16[64,256]{1,0:T(8,128)(2,1)} %constant.17.clone.pair_hbm, bf16[128,256]{1,0:T(8,128)(2,1)} %constant.18.clone.across_hbm), custom_call_target="tpu_custom_call" | custom-call | flops 536870912 | bytes 2097152 | tf_op jit(solution)/shard_map/field_analysis/pallas_call | solution.py:857
  4.5 7.4 %all-to-all-start = ((bf16[16,64,128]{2,1,0:T(8,128)(2,1)}), bf16[16,64,128]{2,1,0:T(8,128)(2,1)S(1)}, u32[]{:S(2)}, u32[]{:S(2)}) async-start(bf16[16,64,128]{2,1,0:T(8,128)(2,1)} %bitcast), calls=%async_computation | async-start | bytes 524288 | tf_op jit(solution)/shard_map/all_to_all | solution.py:835
  11.8 0.0 copy-done.5
  11.8 0.0 copy-start
  11.9 0.0 copy-start.2
  11.9 0.0 copy-start.3
  11.9 4.8 %channel_map.1.point_hbm = bf16[64,2,64,128]{3,2,1,0:T(8,128)(2,1)} custom-call(bf16[64,64]{1,0:T(8,128)(2,1)S(1)} %copy-done.5, bf16[64,2,64,128]{3,2,1,0:T(8,128)(2,1)} %field_hbm.3), custom_call_target="tpu_custom_call" | custom-call | flops 2147483648 | bytes 4194304 | tf_op jit(solution)/shard_map/channel_map/pallas_call | solution.py:840
  16.6 5.2 %all-to-all-done = bf16[16,64,128]{2,1,0:T(8,128)(2,1)S(1)} async-done(((bf16[16,64,128]{2,1,0:T(8,128)(2,1)}), bf16[16,64,128]{2,1,0:T(8,128)(2,1)S(1)}, u32[]{:S(2)}, u32[]{:S(2)}) %all-to-all-start) | async-done | bytes 262176 | tf_op jit(solution)/shard_map/all_to_all | solution.py:835
  21.9 0.0 copy-done
  21.9 0.0 copy-done.2
  21.9 0.0 copy-done.3
  21.9 0.0 copy-start.4
  21.9 7.6 %mode_product.1 = (bf16[16,64,128]{2,1,0:T(8,128)(2,1)}, bf16[1024,128]{1,0:T(8,128)(2,1)S(1)}) custom-call(bf16[1024,128]{1,0:T(8,128)(2,1)S(1)} %bitcast.10, bf16[65536,128]{1,0:T(8,128)(2,1)} %bitcast.14, bf16[128,64]{1,0:T(8,128)(2,1)S(1)} %copy-done.2, bf16[64,64]{1,0:T(8,128)(2,1)S(1)} %copy-done.3, bf16[64,64]{1,0:T(8,128)(2,1)S(1)} %copy-done), custom_call_target="tpu_custom_call" | custom-call | flops 268435456 | bytes 17825792 | tf_op jit(solution)/shard_map/mode_product/pallas_call | solution.py:880
  29.5 12.8 %all_to_all.20 = bf16[16,64,128]{2,1,0:T(8,128)(2,1)S(1)} all-to-all(bf16[16,64,128]{2,1,0:T(8,128)(2,1)S(1)} %bitcast.13), channel_id=1, replica_groups=mesh['grp'=2,'gx'=16] {'gx'}, dimensions={0} | all-to-all | bytes 524288 | tf_op jit(solution)/shard_map/all_to_all | solution.py:835
  42.4 0.0 copy-done.4
  42.4 8.6 %gelu_and_gradient.1 = (bf16[64,2,64,128]{3,2,1,0:T(8,128)(2,1)}, bf16[64,2,64,128]{3,2,1,0:T(8,128)(2,1)}, bf16[1024,128]{1,0:T(8,128)(2,1)}) custom-call(bf16[1024,128]{1,0:T(8,128)(2,1)S(1)} %bitcast.12, f32[64]{0:T(128)S(1)} %copy-done.4, bf16[64,2,64,128]{3,2,1,0:T(8,128)(2,1)} %channel_map.1.point_hbm, bf16[64,2,64,128]{3,2,1,0:T(8,128)(2,1)} %cot_hbm.1, ...), custom_call_target="tpu_custom_call" | custom-call | flops 1073741824 | bytes 8388608 | tf_op jit(solution)/shard_map/gelu_and_gradient/pallas_call | solution.py:901
  51.0 3.5 %all-to-all-start.2 = ((bf16[16,64,128]{2,1,0:T(8,128)(2,1)}), bf16[16,64,128]{2,1,0:T(8,128)(2,1)S(1)}, u32[]{:S(2)}, u32[]{:S(2)}) async-start(bf16[16,64,128]{2,1,0:T(8,128)(2,1)} %bitcast.5), calls=%async_computation.2 | async-start | bytes 524288 | tf_op jit(solution)/shard_map/all_to_all | solution.py:835
  54.5 0.0 copy-start.1
  54.6 4.8 %channel_map_back.1.point_hbm = bf16[64,2,64,128]{3,2,1,0:T(8,128)(2,1)} custom-call(bf16[64,64]{1,0:T(8,128)(2,1)S(1)} %copy-done.5, bf16[64,2,64,128]{3,2,1,0:T(8,128)(2,1)} %get-tuple-element.20.field_hbm), custom_call_target="tpu_custom_call" | custom-call | flops 2147483648 | bytes 4194304 | tf_op jit(solution)/shard_map/channel_map_back/pallas_call | solution.py:840
  59.3 5.2 %all-to-all-done.2 = bf16[16,64,128]{2,1,0:T(8,128)(2,1)S(1)} async-done(((bf16[16,64,128]{2,1,0:T(8,128)(2,1)}), bf16[16,64,128]{2,1,0:T(8,128)(2,1)S(1)}, u32[]{:S(2)}, u32[]{:S(2)}) %all-to-all-start.2) | async-done | bytes 262176 | tf_op jit(solution)/shard_map/all_to_all | solution.py:835
  64.5 0.0 copy-done.1
  64.5 9.3 %mode_gradient.1 = (bf16[32,64,128]{2,1,0:T(8,128)(2,1)S(1)}, bf16[16,64,128]{2,1,0:T(8,128)(2,1)S(1)}, bf16[1024,128]{1,0:T(8,128)(2,1)}) custom-call(bf16[1024,128]{1,0:T(8,128)(2,1)S(1)} %bitcast.9, bf16[65536,128]{1,0:T(8,128)(2,1)} %bitcast.15, bf16[128,64]{1,0:T(8,128)(2,1)S(1)} %copy-done.1, bf16[64,64]{1,0:T(8,128)(2,1)S(1)} %copy-done, ...), custom_call_target="tpu_custom_call" | custom-call | flops 268435456 | bytes 17825792 | tf_op jit(solution)/shard_map/mode_gradient/pallas_call | solution.py:940
  73.9 3.5 %all-to-all-start.3 = ((bf16[16,64,128]{2,1,0:T(8,128)(2,1)}), bf16[16,64,128]{2,1,0:T(8,128)(2,1)S(1)}, u32[]{:S(2)}, u32[]{:S(2)}) async-start(bf16[16,64,128]{2,1,0:T(8,128)(2,1)} %bitcast.7), calls=%async_computation.3 | async-start | bytes 524288 | tf_op jit(solution)/shard_map/all_to_all | solution.py:835
  77.4 9.2 %weight_gradient.1 = bf16[1024,64,128]{2,1,0:T(8,128)(2,1)} custom-call(bf16[16,64,128]{2,1,0:T(8,128)(2,1)S(1)} %get-tuple-element.25.coeff_ref, bf16[32,64,128]{2,1,0:T(8,128)(2,1)S(1)} %get-tuple-element.26.pair_ref), custom_call_target="tpu_custom_call" | custom-call | flops 1073741824 | bytes 17825792 | tf_op jit(solution)/shard_map/weight_gradient/pallas_call | solution.py:963
  86.6 0.8 all-to-all-done.3
  87.4 4.1 %field_gradient.1 = bf16[64,2,64,128]{3,2,1,0:T(8,128)(2,1)} custom-call(bf16[1024,128]{1,0:T(8,128)(2,1)S(1)} %bitcast.11, bf16[64,2,64,128]{3,2,1,0:T(8,128)(2,1)} %channel_map_back.1.point_hbm, bf16[256,1024]{1,0:T(8,128)(2,1)} %constant.16.clone.depth_hbm, bf16[256,128]{1,0:T(8,128)(2,1)} %constant.19.clone.back_hbm), custom_call_target="tpu_custom_call" | custom-call | flops 536870912 | bytes 4194304 | tf_op jit(solution)/shard_map/field_gradient/pallas_call | solution.py:982
Async XLA Ops:
  0.6 11.2 %copy-start.5 = (bf16[64,64]{1,0:T(8,128)(2,1)S(1)}, bf16[64,64]{1,0:T(8,128)(2,1)}, u32[]{:S(2)}) copy-start(bf16[64,64]{1,0:T(8,128)(2,1)} %weight_ref.3) | copy-start | bytes 24580
  4.5 17.4 %all-to-all-start = ((bf16[16,64,128]{2,1,0:T(8,128)(2,1)}), bf16[16,64,128]{2,1,0:T(8,128)(2,1)S(1)}, u32[]{:S(2)}, u32[]{:S(2)}) async-start(bf16[16,64,128]{2,1,0:T(8,128)(2,1)} %bitcast), calls=%async_computation | async-start | bytes 524288 | tf_op jit(solution)/shard_map/all_to_all | solution.py:835
  11.8 10.0 %copy-start = (bf16[64,64]{1,0:T(8,128)(2,1)S(1)}, bf16[64,64]{1,0:T(8,128)(2,1)}, u32[]{:S(2)}) copy-start(bf16[64,64]{1,0:T(8,128)(2,1)} %constant.23.clone.back_ref) | copy-start | bytes 24580
  11.9 10.0 %copy-start.2 = (bf16[128,64]{1,0:T(8,128)(2,1)S(1)}, bf16[128,64]{1,0:T(8,128)(2,1)}, u32[]{:S(2)}) copy-start(bf16[128,64]{1,0:T(8,128)(2,1)} %constant.21.clone.both_ref) | copy-start | bytes 49156
  11.9 10.0 %copy-start.3 = (bf16[64,64]{1,0:T(8,128)(2,1)S(1)}, bf16[64,64]{1,0:T(8,128)(2,1)}, u32[]{:S(2)}) copy-start(bf16[64,64]{1,0:T(8,128)(2,1)} %constant.20.clone.plain_ref) | copy-start | bytes 24580
  21.9 20.5 %copy-start.4 = (f32[64]{0:T(128)S(1)}, f32[64]{0:T(128)}, u32[]{:S(2)}) copy-start(f32[64]{0:T(128)} %bias_ref.1) | copy-start | bytes 772
  51.0 13.6 %all-to-all-start.2 = ((bf16[16,64,128]{2,1,0:T(8,128)(2,1)}), bf16[16,64,128]{2,1,0:T(8,128)(2,1)S(1)}, u32[]{:S(2)}, u32[]{:S(2)}) async-start(bf16[16,64,128]{2,1,0:T(8,128)(2,1)} %bitcast.5), calls=%async_computation.2 | async-start | bytes 524288 | tf_op jit(solution)/shard_map/all_to_all | solution.py:835
  54.5 10.0 %copy-start.1 = (bf16[128,64]{1,0:T(8,128)(2,1)S(1)}, bf16[128,64]{1,0:T(8,128)(2,1)}, u32[]{:S(2)}) copy-start(bf16[128,64]{1,0:T(8,128)(2,1)} %constant.22.clone.straight_ref) | copy-start | bytes 49156
  73.9 13.6 %all-to-all-start.3 = ((bf16[16,64,128]{2,1,0:T(8,128)(2,1)}), bf16[16,64,128]{2,1,0:T(8,128)(2,1)S(1)}, u32[]{:S(2)}, u32[]{:S(2)}) async-start(bf16[16,64,128]{2,1,0:T(8,128)(2,1)} %bitcast.7), calls=%async_computation.3 | async-start | bytes 524288 | tf_op jit(solution)/shard_map/all_to_all | solution.py:835
where the time goes:
time: 92.3 us; the launch traced here: 91.7 us
  Pallas kernels  52.2 us (57%)
  starting transfers between devices  14.5 us (16%)
  blocking collectives  12.8 us (14%)
  waiting for transfers between devices  11.3 us (12%)
  between operations  0.93 us (1%)
    all_to_all x3, starting transfers between devices, exchange(): lax.all_to_all(block.reshape(devices, 64, 128), 'gx', 0, 0, tiled=True)  14.5 us
    all_to_all x1, blocking collectives, exchange(): lax.all_to_all(block.reshape(devices, 64, 128), 'gx', 0, 0, tiled=True)  12.8 us
    all_to_all x3, waiting for transfers between devices, exchange(): lax.all_to_all(block.reshape(devices, 64, 128), 'gx', 0, 0, tiled=True)  11.3 us
    pallas_call x2, Pallas kernels, point(): pl.pallas_call(functools.partial(point_kernel, transposed), out_shape=plt...  9.52 us
    pallas_call x1, Pallas kernels, fast_body(): pl.pallas_call(functools.partial(mode_grad_kernel, forward_scale), out_sh...  9.3 us
    pallas_call x1, Pallas kernels, fast_body(): pl.pallas_call(functools.partial(weight_grad_kernel, weight_scale), out_s...  9.18 us
    pallas_call x1, Pallas kernels, fast_body(): pl.pallas_call(functools.partial(middle_kernel, inverse_scale), out_shape...  8.63 us
    pallas_call x1, Pallas kernels, fast_body(): pl.pallas_call(functools.partial(mode_kernel, forward_scale), out_shape=[...  7.62 us
  transfers between devices with their start and end apart: 3, of which 3 were waited for; matrix products, arithmetic and copies ran while one was open for 0% of the time, Pallas kernels for 20%

commit v1 on v0

--- a/solution.py
+++ b/solution.py
@@ -200,7 +200,8 @@
 STEP = 16
 VMEM_MIB = 32
 VECTOR = 2
-WAITS = {0: 4, 4: 4, 8: 4, 12: 2, 14: 1, 15: 1}
+HEAD = 4
+WAITS = {4: 4, 8: 4, 12: 4}
 NT = (((1,), (1,)), ((), ()))
 F32 = jnp.float32
 BF16 = jnp.bfloat16
@@ -324,25 +325,26 @@
     channels = lines_ref.shape[0] // (2 * MZ)
     across = across_ref[...]
     half = across.shape[0] // 2
-    for kzh in range(MZ // 2):
+    for first in range(0, MZ // 2, 2):
         pair = jnp.concatenate(
             [
                 jnp.concatenate(
                     [
-                        lines_ref[pl.ds(a * MZ + 2 * kzh + h, channels, stride=2 * MZ), :]
+                        lines_ref[pl.ds(a * MZ + kz, channels, stride=2 * MZ), :]
                         for a in range(2)
                     ],
                     axis=1,
                 )
-                for h in range(2)
+                for kz in range(2 * first, 2 * first + 4)
             ],
             axis=0,
         ).astype(BF16)
         rows = dot_nt(across, pair)
-        for kyl in range(2):
-            rows_ref[pl.ds(kyl * 8 + kzh, half, stride=16), :] = rows[
-                kyl * half : (kyl + 1) * half
-            ]
+        for k in range(2):
+            for kyl in range(2):
+                rows_ref[pl.ds(kyl * 8 + first + k, half, stride=16), :] = rows[
+                    kyl * half : (kyl + 1) * half, k * 128 : (k + 1) * 128
+                ]
     out_ref[...] = rows_ref[...].astype(BF16)
 
 
@@ -350,15 +352,23 @@
     rows_ref[...] = block_ref[...].astype(F32)
     count = rows_ref.shape[0] // 16
     eye = (sublanes((128, 128)) == lanes((128, 128))).astype(BF16)
-    for kzh in range(MZ // 2):
+    for first in range(0, MZ // 2, 2):
         both = jnp.concatenate(
-            [rows_ref[pl.ds(kyl * 8 + kzh, count, stride=16), :] for kyl in range(2)], axis=0
+            [
+                rows_ref[pl.ds(kyl * 8 + first + k, count, stride=16), :]
+                for k in range(2)
+                for kyl in range(2)
+            ],
+            axis=0,
         ).astype(BF16)
         turned = dot_nt(eye, both)
-        for h in range(2):
-            spec_ref[:, (2 * kzh + h) * GROUP : (2 * kzh + h + 1) * GROUP, :] = turned[
-                h * 64 : (h + 1) * 64
-            ].reshape(8, GROUP, turned.shape[1])
+        half = turned.shape[1] // 2
+        for k in range(2):
+            for h in range(2):
+                at = (2 * (first + k) + h) * GROUP
+                spec_ref[:, at : at + GROUP, :] = turned[
+                    h * 64 : (h + 1) * 64, k * half : (k + 1) * half
+                ].reshape(8, GROUP, half)
 
 
 def lines_synthesis(step, spec_ref, back, scale):
@@ -526,24 +536,49 @@
     for copy in tables_in:
         copy.wait()
     steps = point_ref.shape[0] // STEP
-
-    @pl.loop(0, steps)
-    def _(step):
-        part_copy(point_hbm, point_ref, point_sems, step, STEP).wait()
-        for g, wide in enumerate(lines_synthesis(step, spec_ref, back_ref[...], None)):
-            spectral = dot_nn(wide, depth_ref[...])
-            for ci in range(GROUP):
-                index = (step * (STEP // GROUP) + g) * GROUP + ci
-                total = spectral[:, ci * 128 : (ci + 1) * 128] + flat(point_ref[index]).astype(F32)
+    groups = point_ref.shape[0] // GROUP
+    per_step = STEP // GROUP
+
+    def quarter(wide, at):
+        return dot_nn(wide, depth_ref[:, at * 256 : (at + 1) * 256])
+
+    wides = lines_synthesis(0, spec_ref, back_ref[...], None)
+    spectral = [quarter(wides[0], at) for at in range(4)]
+    for group in range(groups):
+        step = group // per_step
+        if group % per_step == 0:
+            part_copy(point_hbm, point_ref, point_sems, step, STEP).wait()
+            if step + 1 < steps:
+                wides += lines_synthesis(step + 1, spec_ref, back_ref[...], None)
+        following = []
+        for at in range(4):
+            if group + 1 < groups:
+                following.append(quarter(wides[group + 1], at))
+            for k in range(2):
+                index = group * GROUP + 2 * at + k
+                total = spectral[at][:, k * 128 : (k + 1) * 128] + flat(point_ref[index]).astype(F32)
                 out_ref[index] = total.astype(BF16).reshape(out_ref.shape[1:])
-        part_copy(out_ref, out_hbm, out_sems, step, STEP).start()
+        if group % per_step == per_step - 1:
+            part_copy(out_ref, out_hbm, out_sems, step, STEP).start()
+        spectral = following
 
     for step in range(steps):
         part_copy(out_ref, out_hbm, out_sems, step, STEP).wait()
 
 
 def point_kernel(
-    transposed, weight_ref, field_hbm, out_hbm, field_ref, out_ref, wide_ref, in_sems, out_sems
+    transposed,
+    weight_ref,
+    field_hbm,
+    modes_hbm,
+    out_hbm,
+    head_ref,
+    field_ref,
+    out_ref,
+    wide_ref,
+    in_sems,
+    out_sems,
+    head_sems,
 ):
     size = wide_ref.shape[0]
     planes = field_ref.shape[1]
@@ -553,6 +588,7 @@
         copy = pltpu.make_async_copy(field_hbm.at[part], field_ref.at[part], in_sems.at[plane])
         copy.start()
         copies.append(copy)
+    heads = start_weights(modes_hbm, head_ref, head_sems, 0)
     tall = (sublanes((size, 64)) // 16 == lanes((size, 64))).astype(BF16)
     weight = weight_ref[...]
     left = dot_nt(tall, weight) if transposed else dot_nn(tall, weight)
@@ -585,25 +621,29 @@
         copy = pltpu.make_async_copy(out_ref.at[part], out_hbm.at[part], out_sems.at[plane])
         copy.start()
         sends.append(copy)
-    for copy in sends:
+    for copy in sends + heads:
         copy.wait()
 
 
-def start_weights(weight_hbm, weight_ref, sems):
+def start_weights(weight_hbm, weight_ref, sems, first):
+    rows = weight_hbm.shape[0] // 16
     copies = []
-    for j in range(16):
-        rows = weight_ref.shape[0] // 16
-        part = pl.ds(j * rows, rows)
-        copy = pltpu.make_async_copy(weight_hbm.at[part], weight_ref.at[part], sems.at[j])
+    for index in range(weight_ref.shape[0] // rows):
+        copy = pltpu.make_async_copy(
+            weight_hbm.at[pl.ds((first + index) * rows, rows)],
+            weight_ref.at[pl.ds(index * rows, rows)],
+            sems.at[index],
+        )
         copy.start()
         copies.append(copy)
     return copies
 
 
-def mode_pair(weight_ref, j, h, u):
-    start = ((j * 2 + h) * MX + 8 * u) * 64
+def mode_pair(head_ref, weight_ref, j, h, u):
+    source = head_ref if j < HEAD else weight_ref
+    start = (((j if j < HEAD else j - HEAD) * 2 + h) * MX + 8 * u) * 64
     return jnp.concatenate(
-        [weight_ref[start : start + 256, :], weight_ref[start + 256 : start + 512, :]], axis=1
+        [source[start : start + 256, :], source[start + 256 : start + 512, :]], axis=1
     )
 
 
@@ -618,6 +658,7 @@
 def mode_kernel(
     scale,
     block_ref,
+    head_ref,
     weight_hbm,
     both_ref,
     plain_ref,
@@ -633,7 +674,7 @@
     sems,
     coeff_sems,
 ):
-    copies = start_weights(weight_hbm, weight_ref, sems)
+    copies = start_weights(weight_hbm, weight_ref, sems, HEAD)
     count = rows_ref.shape[0] // 16
     rows_ref[...] = block_ref[...].astype(F32)
     low = lanes((128, 128)) < 64
@@ -660,12 +701,12 @@
     send = pltpu.make_async_copy(coeff_ref, coeff_hbm, coeff_sems.at[0])
     send.start()
     for j in range(16):
-        for copy in copies[j : j + WAITS.get(j, 0)]:
+        for copy in copies[j - HEAD : j - HEAD + WAITS.get(j, 0)]:
             copy.wait()
         mixed = []
         for u in range(MX // 8):
             halves = [
-                dot_nn(left_ref[j, h, u * 32 : (u + 1) * 32, :], mode_pair(weight_ref, j, h, u))
+                dot_nn(left_ref[j, h, u * 32 : (u + 1) * 32, :], mode_pair(head_ref, weight_ref, j, h, u))
                 for h in range(2)
             ]
             for t in range(2):
@@ -685,6 +726,7 @@
 def mode_grad_kernel(
     scale,
     block_ref,
+    head_ref,
     weight_hbm,
     straight_ref,
     back_ref,
@@ -701,7 +743,7 @@
 ):
     send = pltpu.make_async_copy(coeff_hbm, coeff_ref, coeff_sems.at[0])
     send.start()
-    copies = start_weights(weight_hbm, weight_ref, sems)
+    copies = start_weights(weight_hbm, weight_ref, sems, HEAD)
     count = rows_ref.shape[0] // 16
     rows_ref[...] = block_ref[...].astype(F32)
     low = lanes((64, 128)) < 64
@@ -722,7 +764,7 @@
             part = turned[:, h * 128 : (h + 1) * 128]
             pair_ref[2 * j + h] = jnp.where(low, part[:64], part[64:]).astype(BF16)
     for j in range(16):
-        for copy in copies[j : j + WAITS.get(j, 0)]:
+        for copy in copies[j - HEAD : j - HEAD + WAITS.get(j, 0)]:
             copy.wait()
         mixed = []
         for u in range(MX // 8):
@@ -731,15 +773,15 @@
                 pair = pair_ref[2 * j + h, u * 16 : (u + 1) * 16, :]
                 rows = dot_nt(
                     jnp.concatenate([pair * even, pair * odd], axis=1),
-                    mode_pair(weight_ref, j, h, u),
+                    mode_pair(head_ref, weight_ref, j, h, u),
                 )
                 found.append(jnp.where(valid, jnp.where(upper, rows[:, :128], rows[:, 128:]), 0.0))
             keep = jnp.where(low16, found[0], found[1])
             move = jnp.where(low16, found[1], found[0])
             mixed.append(keep + swap_halves(move))
         mixed_ref[j] = (jnp.concatenate(mixed, axis=0) * scale).astype(BF16)
-        if j % 4 == 3:
-            plane_sums(back_ref, mixed_ref, res_ref, j // 4)
+    for quarter in range(4):
+        plane_sums(back_ref, mixed_ref, res_ref, quarter)
     out_ref[...] = res_ref[...].astype(BF16)
     send.wait()
 
@@ -822,6 +864,9 @@
     def in_hbm(array):
         return pltpu.with_memory_space_constraint(array, pltpu.HBM)
 
+    def in_vmem(array):
+        return pltpu.with_memory_space_constraint(array, pltpu.VMEM)
+
     steps = channels // STEP
     lines_scratch = pltpu.VMEM((channels * 2 * MZ, planes * lines), F32)
     rows_scratch = pltpu.VMEM((block_rows, 128), F32)
@@ -839,20 +884,24 @@
     def point(field, transposed):
         return pl.pallas_call(
             functools.partial(point_kernel, transposed),
-            out_shape=pltpu.HBM(features.shape, BF16),
-            in_specs=[vmem, hbm],
-            out_specs=hbm,
+            out_shape=[
+                pltpu.HBM(features.shape, BF16),
+                pltpu.VMEM((weight_rows.shape[0] * HEAD // 16, weight_rows.shape[1]), BF16),
+            ],
+            in_specs=[vmem, hbm, hbm],
+            out_specs=[hbm, vmem],
             scratch_shapes=[
                 field_scratch,
                 field_scratch,
                 pltpu.VMEM((channels * 16, channels * 16), BF16),
                 sems(planes),
                 sems(planes),
+                sems(HEAD),
             ],
             compiler_params=params(VMEM_MIB),
             cost_estimate=cost(2 * 1024**3, 2 * field_bytes),
             name="channel_map_back" if transposed else "channel_map",
-        )(channel_weight, in_hbm(field))
+        )(channel_weight, in_hbm(field), weight_rows)
 
     block = pl.pallas_call(
         analysis_kernel,
@@ -872,15 +921,18 @@
         cost_estimate=cost(2 * 256 * 1024 * 1024, field_bytes),
         name="field_analysis",
     )(in_hbm(features), table["depth_pair"], table["across_y"])
-    block, pointwise = lax.optimization_barrier((exchange(block), point(features, False)))
-
-    weight_scratch = pltpu.VMEM(weight_rows.shape, BF16)
+    pointwise, head = point(features, False)
+    block, pointwise, head = lax.optimization_barrier((exchange(block), pointwise, head))
+
+    weight_scratch = pltpu.VMEM(
+        (weight_rows.shape[0] * (16 - HEAD) // 16, weight_rows.shape[1]), BF16
+    )
     mixed_scratch = pltpu.VMEM((16, 64, 128), BF16)
-    weight_sems = sems(16)
+    weight_sems = sems(16 - HEAD)
     coeffs, block = pl.pallas_call(
         functools.partial(mode_kernel, forward_scale),
         out_shape=[pltpu.HBM((16, 64, 128), BF16), block_shape],
-        in_specs=[vmem, hbm, vmem, vmem, vmem],
+        in_specs=[vmem, vmem, hbm, vmem, vmem, vmem],
         out_specs=[hbm, vmem],
         scratch_shapes=[
             pltpu.VMEM((16, 64, 128), BF16),
@@ -895,7 +947,7 @@
         compiler_params=params(VMEM_MIB),
         cost_estimate=cost(256 * 2 * 16 * 256 * 128, 17 * 2**20),
         name="mode_product",
-    )(block, weight_rows, table["both_x"], table["plain_x"], table["back_x"])
+    )(block, in_vmem(head), weight_rows, table["both_x"], table["plain_x"], table["back_x"])
     block = exchange(block)
 
     activated, upstream, block = pl.pallas_call(
@@ -934,8 +986,8 @@
         table["across_y"],
         table["back_y"],
     )
-    block = exchange(block)
-    block, channel_back = lax.optimization_barrier((block, point(upstream, True)))
+    channel_back, head = point(upstream, True)
+    block, channel_back, head = lax.optimization_barrier((exchange(block), channel_back, head))
 
     pairs, coeffs, block = pl.pallas_call(
         functools.partial(mode_grad_kernel, forward_scale),
@@ -944,7 +996,7 @@
             pltpu.VMEM((16, 64, 128), BF16),
             block_shape,
         ],
-        in_specs=[vmem, hbm, vmem, vmem, hbm],
+        in_specs=[vmem, vmem, hbm, vmem, vmem, hbm],
         out_specs=[vmem, vmem, vmem],
         scratch_shapes=[
             weight_scratch,
@@ -957,7 +1009,7 @@
         compiler_params=params(VMEM_MIB),
         cost_estimate=cost(256 * 2 * 16 * 256 * 128, 17 * 2**20),
         name="mode_gradient",
-    )(block, weight_rows, table["straight_x"], table["back_x"], in_hbm(coeffs))
+    )(block, in_vmem(head), weight_rows, table["straight_x"], table["back_x"], in_hbm(coeffs))
     block = exchange(block)
 
     spectral_grad = pl.pallas_call(
@@ -975,8 +1027,8 @@
         cost_estimate=cost(512 * 2 * 64 * 64 * 256, 17 * 2**20),
         name="weight_gradient",
     )(
-        pltpu.with_memory_space_constraint(coeffs, pltpu.VMEM),
-        pltpu.with_memory_space_constraint(pairs, pltpu.VMEM),
+        in_vmem(coeffs),
+        in_vmem(pairs),
     )
 
     feature_grad = pl.pallas_call(

time: 92.3 us -> 94.1 us (1.020)
  local copies, waits for them, and re-layouts: 0.04 us -> 8.42 us
  waiting for transfers between devices: 11.3 us -> 5.93 us
  Pallas kernels: 52.2 us -> 50.5 us
    unnamed x12 -> x20, local copies, waits for them, and re-layouts: 0.04 us -> 8.42 us
    all_to_all x3, waiting for transfers between devices: 11.3 us -> 5.93 us  [exchange(): lax.all_to_all(block.reshape(devices, 64, 128), 'gx', 0, 0, tiled=True)]
    pallas_call x1, Pallas kernels: 9.3 us -> 7.94 us  [fast_body(): pl.pallas_call(functools.partial(mode_grad_kernel, forward_scale), out_sh...]
    pallas_call x1, Pallas kernels: 7.62 us -> 6.28 us  [fast_body(): pl.pallas_call(functools.partial(mode_kernel, forward_scale), out_shape=[...]
    pallas_call x2, Pallas kernels: 9.52 us -> 10.8 us  [point(): pl.pallas_call(functools.partial(point_kernel, transposed), out_shape=[pl...]
  transfers between devices with their start and end apart: 3 -> 3, of which waited for: 3 -> 3; matrix products, arithmetic and copies ran while one was open for 0% -> 0% of each run, Pallas kernels for 20% -> 21%
where the time goes in v1:
time: 94.1 us; the launch traced here: 93.5 us
  Pallas kernels  50.5 us (54%)
  starting transfers between devices  14.5 us (15%)
  blocking collectives  13.3 us (14%)
  local copies, waits for them, and re-layouts  8.42 us (9%)
  waiting for transfers between devices  5.93 us (6%)
  between operations  0.95 us (1%)
    all_to_all x3, starting transfers between devices, exchange(): lax.all_to_all(block.reshape(devices, 64, 128), 'gx', 0, 0, tiled=True)  14.5 us
    all_to_all x1, blocking collectives, exchange(): lax.all_to_all(block.reshape(devices, 64, 128), 'gx', 0, 0, tiled=True)  13.3 us
    pallas_call x2, Pallas kernels, point(): pl.pallas_call(functools.partial(point_kernel, transposed), out_shape=[pl...  10.8 us
    pallas_call x1, Pallas kernels, fast_body(): pl.pallas_call(functools.partial(weight_grad_kernel, weight_scale), out_s...  9.18 us
    pallas_call x1, Pallas kernels, fast_body(): pl.pallas_call(functools.partial(middle_kernel, inverse_scale), out_shape...  8.63 us
    unnamed x20, local copies, waits for them, and re-layouts  8.42 us
    pallas_call x1, Pallas kernels, fast_body(): pl.pallas_call(functools.partial(mode_grad_kernel, forward_scale), out_sh...  7.94 us
    pallas_call x1, Pallas kernels, fast_body(): pl.pallas_call(functools.partial(mode_kernel, forward_scale), out_shape=[...  6.28 us
  transfers between devices with their start and end apart: 3, of which 3 were waited for; matrix products, arithmetic and copies ran while one was open for 0% of the time, Pallas kernels for 21%

profile of v1, /device:TPU:0, one launch (start us, length us, event | category | flops | bytes accessed | tf_op | source)
XLA Modules:
  0.0 93.5 jit_solution(2487097046888619158)
XLA Ops:
  0.6 0.0 copy-start.5
  0.6 3.7 %field_analysis.1 = bf16[1024,128]{1,0:T(8,128)(2,1)} custom-call(bf16[64,2,64,128]{3,2,1,0:T(8,128)(2,1)} %field_hbm.3, bf16[64,256]{1,0:T(8,128)(2,1)} %constant.17.clone.pair_hbm, bf16[128,256]{1,0:T(8,128)(2,1)} %constant.18.clone.across_hbm), custom_call_target="tpu_custom_call" | custom-call | flops 536870912 | bytes 2097152 | tf_op jit(solution)/shard_map/field_analysis/pallas_call | solution.py:906
  4.4 7.4 %all-to-all-start = ((bf16[16,64,128]{2,1,0:T(8,128)(2,1)}), bf16[16,64,128]{2,1,0:T(8,128)(2,1)S(1)}, u32[]{:S(2)}, u32[]{:S(2)}) async-start(bf16[16,64,128]{2,1,0:T(8,128)(2,1)} %bitcast), calls=%async_computation | async-start | bytes 524288 | tf_op jit(solution)/shard_map/all_to_all | solution.py:880
  11.8 0.0 copy-done.5
  11.8 0.0 copy-start.4
  11.8 0.0 copy-start.7
  11.8 0.0 copy-start.8
  11.8 5.4 %channel_map.1 = (bf16[64,2,64,128]{3,2,1,0:T(8,128)(2,1)}, bf16[16384,128]{1,0:T(8,128)(2,1)S(1)}) custom-call(bf16[64,64]{1,0:T(8,128)(2,1)S(1)} %copy-done.5, bf16[64,2,64,128]{3,2,1,0:T(8,128)(2,1)} %field_hbm.3, bf16[65536,128]{1,0:T(8,128)(2,1)} %bitcast.14), custom_call_target="tpu_custom_call" | custom-call | flops 2147483648 | bytes 4194304 | tf_op jit(solution)/shard_map/channel_map/pallas_call | solution.py:885
  17.2 0.0 copy-start.2
  17.3 2.0 %copy-done.2 = bf16[16384,128]{1,0:T(8,128)(2,1)} copy-done((bf16[16384,128]{1,0:T(8,128)(2,1)}, bf16[16384,128]{1,0:T(8,128)(2,1)S(1)}, u32[]{:S(2)}) %copy-start.2) | copy-done | bytes 4194328
  19.3 2.6 %all-to-all-done = bf16[16,64,128]{2,1,0:T(8,128)(2,1)S(1)} async-done(((bf16[16,64,128]{2,1,0:T(8,128)(2,1)}), bf16[16,64,128]{2,1,0:T(8,128)(2,1)S(1)}, u32[]{:S(2)}, u32[]{:S(2)}) %all-to-all-start) | async-done | bytes 262176 | tf_op jit(solution)/shard_map/all_to_all | solution.py:880
  21.8 0.0 copy-done.4
  21.8 0.0 copy-done.7
  21.8 0.0 copy-done.8
  21.8 0.0 copy-start.3
  21.8 2.2 %copy-done.3 = bf16[16384,128]{1,0:T(8,128)(2,1)S(1)} copy-done((bf16[16384,128]{1,0:T(8,128)(2,1)S(1)}, bf16[16384,128]{1,0:T(8,128)(2,1)}, u32[]{:S(2)}) %copy-start.3) | copy-done | bytes 4194328
  24.0 6.3 %mode_product.1 = (bf16[16,64,128]{2,1,0:T(8,128)(2,1)}, bf16[1024,128]{1,0:T(8,128)(2,1)S(1)}) custom-call(bf16[1024,128]{1,0:T(8,128)(2,1)S(1)} %bitcast.12, bf16[16384,128]{1,0:T(8,128)(2,1)S(1)} %copy-done.3, bf16[65536,128]{1,0:T(8,128)(2,1)} %bitcast.15, bf16[128,64]{1,0:T(8,128)(2,1)S(1)} %copy-done.7, bf16[64,64]{1,0:T(8,128)(2,1)S(1)} %copy-done.8, ...), custom_call_target="tpu_custom_call" | custom-call | flops 268435456 | bytes 17825792 | tf_op jit(solution)/shard_map/mode_product/pallas_call | solution.py:932
  30.3 13.3 %all_to_all.20 = bf16[16,64,128]{2,1,0:T(8,128)(2,1)S(1)} all-to-all(bf16[16,64,128]{2,1,0:T(8,128)(2,1)S(1)} %bitcast.13), channel_id=1, replica_groups=mesh['grp'=2,'gx'=16] {'gx'}, dimensions={0} | all-to-all | bytes 524288 | tf_op jit(solution)/shard_map/all_to_all | solution.py:880
  43.6 0.0 copy-done.9
  43.6 8.6 %gelu_and_gradient.1 = (bf16[64,2,64,128]{3,2,1,0:T(8,128)(2,1)}, bf16[64,2,64,128]{3,2,1,0:T(8,128)(2,1)}, bf16[1024,128]{1,0:T(8,128)(2,1)}) custom-call(bf16[1024,128]{1,0:T(8,128)(2,1)S(1)} %bitcast.11, f32[64]{0:T(128)S(1)} %copy-done.9, bf16[64,2,64,128]{3,2,1,0:T(8,128)(2,1)} %get-tuple-element.26.point_hbm, bf16[64,2,64,128]{3,2,1,0:T(8,128)(2,1)} %cot_hbm.1, ...), custom_call_target="tpu_custom_call" | custom-call | flops 1073741824 | bytes 8388608 | tf_op jit(solution)/shard_map/gelu_and_gradient/pallas_call | solution.py:953
  52.3 3.5 %all-to-all-start.2 = ((bf16[16,64,128]{2,1,0:T(8,128)(2,1)}), bf16[16,64,128]{2,1,0:T(8,128)(2,1)S(1)}, u32[]{:S(2)}, u32[]{:S(2)}) async-start(bf16[16,64,128]{2,1,0:T(8,128)(2,1)} %bitcast.5), calls=%async_computation.2 | async-start | bytes 524288 | tf_op jit(solution)/shard_map/all_to_all | solution.py:880
  55.8 0.0 copy-start.6
  55.8 5.4 %channel_map_back.1 = (bf16[64,2,64,128]{3,2,1,0:T(8,128)(2,1)}, bf16[16384,128]{1,0:T(8,128)(2,1)S(1)}) custom-call(bf16[64,64]{1,0:T(8,128)(2,1)S(1)} %copy-done.5, bf16[64,2,64,128]{3,2,1,0:T(8,128)(2,1)} %get-tuple-element.29.field_hbm, bf16[65536,128]{1,0:T(8,128)(2,1)} %bitcast.16), custom_call_target="tpu_custom_call" | custom-call | flops 2147483648 | bytes 4194304 | tf_op jit(solution)/shard_map/channel_map_back/pallas_call | solution.py:885
  61.2 0.0 copy-start
  61.3 2.0 %copy-done = bf16[16384,128]{1,0:T(8,128)(2,1)} copy-done((bf16[16384,128]{1,0:T(8,128)(2,1)}, bf16[16384,128]{1,0:T(8,128)(2,1)S(1)}, u32[]{:S(2)}) %copy-start) | copy-done | bytes 4194328
  63.3 2.6 %all-to-all-done.2 = bf16[16,64,128]{2,1,0:T(8,128)(2,1)S(1)} async-done(((bf16[16,64,128]{2,1,0:T(8,128)(2,1)}), bf16[16,64,128]{2,1,0:T(8,128)(2,1)S(1)}, u32[]{:S(2)}, u32[]{:S(2)}) %all-to-all-start.2) | async-done | bytes 262176 | tf_op jit(solution)/shard_map/all_to_all | solution.py:880
  65.8 2.2 %copy-done.1 = bf16[16384,128]{1,0:T(8,128)(2,1)S(1)} copy-done((bf16[16384,128]{1,0:T(8,128)(2,1)S(1)}, bf16[16384,128]{1,0:T(8,128)(2,1)}, u32[]{:S(2)}) %copy-start.1) | copy-done | bytes 4194328
  68.0 7.9 %mode_gradient.1 = (bf16[32,64,128]{2,1,0:T(8,128)(2,1)S(1)}, bf16[16,64,128]{2,1,0:T(8,128)(2,1)S(1)}, bf16[1024,128]{1,0:T(8,128)(2,1)}) custom-call(bf16[1024,128]{1,0:T(8,128)(2,1)S(1)} %bitcast.9, bf16[16384,128]{1,0:T(8,128)(2,1)S(1)} %copy-done.1, bf16[65536,128]{1,0:T(8,128)(2,1)} %bitcast.17, bf16[128,64]{1,0:T(8,128)(2,1)S(1)} %copy-done.6, ...), custom_call_target="tpu_custom_call" | custom-call | flops 268435456 | bytes 17825792 | tf_op jit(solution)/shard_map/mode_gradient/pallas_call | solution.py:992
  76.0 3.5 %all-to-all-start.3 = ((bf16[16,64,128]{2,1,0:T(8,128)(2,1)}), bf16[16,64,128]{2,1,0:T(8,128)(2,1)S(1)}, u32[]{:S(2)}, u32[]{:S(2)}) async-start(bf16[16,64,128]{2,1,0:T(8,128)(2,1)} %bitcast.7), calls=%async_computation.3 | async-start | bytes 524288 | tf_op jit(solution)/shard_map/all_to_all | solution.py:880
  79.5 9.2 %weight_gradient.1 = bf16[1024,64,128]{2,1,0:T(8,128)(2,1)} custom-call(bf16[16,64,128]{2,1,0:T(8,128)(2,1)S(1)} %get-tuple-element.37.coeff_ref, bf16[32,64,128]{2,1,0:T(8,128)(2,1)S(1)} %get-tuple-element.38.pair_ref), custom_call_target="tpu_custom_call" | custom-call | flops 1073741824 | bytes 17825792 | tf_op jit(solution)/shard_map/weight_gradient/pallas_call | solution.py:1015
  88.7 0.8 all-to-all-done.3
  89.5 3.9 %field_gradient.1 = bf16[64,2,64,128]{3,2,1,0:T(8,128)(2,1)} custom-call(bf16[1024,128]{1,0:T(8,128)(2,1)S(1)} %bitcast.10, bf16[64,2,64,128]{3,2,1,0:T(8,128)(2,1)} %get-tuple-element.36.point_hbm, bf16[256,1024]{1,0:T(8,128)(2,1)} %constant.16.clone.depth_hbm, bf16[256,128]{1,0:T(8,128)(2,1)} %constant.19.clone.back_hbm), custom_call_target="tpu_custom_call" | custom-call | flops 536870912 | bytes 4194304 | tf_op jit(solution)/shard_map/field_gradient/pallas_call | solution.py:1034
  (3 shorter events, 0.0 us)
Async XLA Ops:
  0.6 11.1 %copy-start.5 = (bf16[64,64]{1,0:T(8,128)(2,1)S(1)}, bf16[64,64]{1,0:T(8,128)(2,1)}, u32[]{:S(2)}) copy-start(bf16[64,64]{1,0:T(8,128)(2,1)} %weight_ref.3) | copy-start | bytes 24580
  4.4 17.4 %all-to-all-start = ((bf16[16,64,128]{2,1,0:T(8,128)(2,1)}), bf16[16,64,128]{2,1,0:T(8,128)(2,1)S(1)}, u32[]{:S(2)}, u32[]{:S(2)}) async-start(bf16[16,64,128]{2,1,0:T(8,128)(2,1)} %bitcast), calls=%async_computation | async-start | bytes 524288 | tf_op jit(solution)/shard_map/all_to_all | solution.py:880
  11.8 10.0 %copy-start.4 = (bf16[64,64]{1,0:T(8,128)(2,1)S(1)}, bf16[64,64]{1,0:T(8,128)(2,1)}, u32[]{:S(2)}) copy-start(bf16[64,64]{1,0:T(8,128)(2,1)} %constant.23.clone.back_ref) | copy-start | bytes 24580
  11.8 10.0 %copy-start.7 = (bf16[128,64]{1,0:T(8,128)(2,1)S(1)}, bf16[128,64]{1,0:T(8,128)(2,1)}, u32[]{:S(2)}) copy-start(bf16[128,64]{1,0:T(8,128)(2,1)} %constant.21.clone.both_ref) | copy-start | bytes 49156
  11.8 10.0 %copy-start.8 = (bf16[64,64]{1,0:T(8,128)(2,1)S(1)}, bf16[64,64]{1,0:T(8,128)(2,1)}, u32[]{:S(2)}) copy-start(bf16[64,64]{1,0:T(8,128)(2,1)} %constant.20.clone.plain_ref) | copy-start | bytes 24580
  17.2 2.0 %copy-start.2 = (bf16[16384,128]{1,0:T(8,128)(2,1)}, bf16[16384,128]{1,0:T(8,128)(2,1)S(1)}, u32[]{:S(2)}) copy-start(bf16[16384,128]{1,0:T(8,128)(2,1)S(1)} %get-tuple-element.24.head_ref) | copy-start | bytes 12582916
  21.8 2.2 %copy-start.3 = (bf16[16384,128]{1,0:T(8,128)(2,1)S(1)}, bf16[16384,128]{1,0:T(8,128)(2,1)}, u32[]{:S(2)}) copy-start(bf16[16384,128]{1,0:T(8,128)(2,1)} %copy-done.2) | copy-start | bytes 12582916
  24.0 19.6 %copy-start.9 = (f32[64]{0:T(128)S(1)}, f32[64]{0:T(128)}, u32[]{:S(2)}) copy-start(f32[64]{0:T(128)} %bias_ref.1) | copy-start | bytes 772
  52.3 13.6 %all-to-all-start.2 = ((bf16[16,64,128]{2,1,0:T(8,128)(2,1)}), bf16[16,64,128]{2,1,0:T(8,128)(2,1)S(1)}, u32[]{:S(2)}, u32[]{:S(2)}) async-start(bf16[16,64,128]{2,1,0:T(8,128)(2,1)} %bitcast.5), calls=%async_computation.2 | async-start | bytes 524288 | tf_op jit(solution)/shard_map/all_to_all | solution.py:880
  55.8 10.0 %copy-start.6 = (bf16[128,64]{1,0:T(8,128)(2,1)S(1)}, bf16[128,64]{1,0:T(8,128)(2,1)}, u32[]{:S(2)}) copy-start(bf16[128,64]{1,0:T(8,128)(2,1)} %constant.22.clone.straight_ref) | copy-start | bytes 49156
  61.2 2.0 %copy-start = (bf16[16384,128]{1,0:T(8,128)(2,1)}, bf16[16384,128]{1,0:T(8,128)(2,1)S(1)}, u32[]{:S(2)}) copy-start(bf16[16384,128]{1,0:T(8,128)(2,1)S(1)} %get-tuple-element.33.head_ref) | copy-start | bytes 12582916
  65.8 2.2 %copy-start.1 = (bf16[16384,128]{1,0:T(8,128)(2,1)S(1)}, bf16[16384,128]{1,0:T(8,128)(2,1)}, u32[]{:S(2)}) copy-start(bf16[16384,128]{1,0:T(8,128)(2,1)} %copy-done) | copy-start | bytes 12582916
  76.0 13.6 %all-to-all-start.3 = ((bf16[16,64,128]{2,1,0:T(8,128)(2,1)}), bf16[16,64,128]{2,1,0:T(8,128)(2,1)S(1)}, u32[]{:S(2)}, u32[]{:S(2)}) async-start(bf16[16,64,128]{2,1,0:T(8,128)(2,1)} %bitcast.7), calls=%async_computation.3 | async-start | bytes 524288 | tf_op jit(solution)/shard_map/all_to_all | solution.py:880

commit v2 on v1

--- a/solution.py
+++ b/solution.py
@@ -200,8 +200,8 @@
 STEP = 16
 VMEM_MIB = 32
 VECTOR = 2
-HEAD = 4
-WAITS = {4: 4, 8: 4, 12: 4}
+HEAD = 2
+WAITS = {2: 2, 4: 4, 8: 4, 12: 4}
 NT = (((1,), (1,)), ((), ()))
 F32 = jnp.float32
 BF16 = jnp.bfloat16
@@ -408,8 +408,7 @@
     start_parts(field_hbm, field_ref, field_sems, STEP)
     first.wait()
 
-    @pl.loop(0, field_ref.shape[0] // STEP)
-    def _(step):
+    for step in range(field_ref.shape[0] // STEP):
         part_copy(field_hbm, field_ref, field_sems, step, STEP).wait()
         for g in range(STEP // GROUP):
             group = step * (STEP // GROUP) + g
@@ -786,23 +785,26 @@
     send.wait()
 
 
-def weight_grad_kernel(scale, coeff_ref, pair_ref, out_hbm, out_ref, mask_ref, pairs_ref, sems):
+def weight_grad_kernel(
+    scale, coeff_ref, pair_ref, out_hbm, out_ref, mask_ref, turned_ref, pairs_ref, sems
+):
     lane = lanes((128, 64))
     part = sublanes((128, 64)) // 64
     for t in range(MX // 4 - VECTOR):
         mask_ref[t] = ((lane // 8 == t) & (lane % 4 // 2 == part)).astype(BF16)
     eye = (sublanes((128, 128)) == lanes((128, 128))).astype(BF16)
+    for j in range(16):
+        turned_ref[j] = (dot_nt(eye, coeff_ref[j]) * scale).astype(BF16)
+        for h in range(2):
+            pairs_ref[2 * j + h] = pair_ref[2 * j + h].astype(F32)
     even = (sublanes((64, 128)) % 2 == 0).astype(BF16)
     odd = (sublanes((64, 128)) % 2 == 1).astype(BF16)
 
-    @pl.loop(0, 16)
-    def _(j):
-        turned = (dot_nt(eye, coeff_ref[j]) * scale).astype(BF16)
+    def one_pair(j):
         for h in range(2):
-            one = turned[h * 64 : (h + 1) * 64]
+            one = turned_ref[j, h * 64 : (h + 1) * 64, :]
             left = jnp.concatenate([one, one], axis=0)
             pair = pair_ref[j * 2 + h]
-            pairs_ref[h] = pair.astype(F32)
             right = jnp.concatenate([pair * even, pair * odd], axis=1)
             for t in range(MX // 4):
                 mode = (j * 2 + h) * MX + 4 * t
@@ -818,10 +820,17 @@
                     for b in range(2):
                         at = t * 8 + b * 4 + k
                         column = jnp.broadcast_to(one[:, at : at + 1], (64, 128))
-                        row = jnp.broadcast_to(pairs_ref[h, at : at + 1, :], (64, 128)).astype(BF16)
+                        row = jnp.broadcast_to(
+                            pairs_ref[j * 2 + h, at : at + 1, :], (64, 128)
+                        ).astype(BF16)
                         total = column * row if total is None else total + column * row
                     out_ref[mode + k] = total
         part_copy(out_ref, out_hbm, sems, j, 2 * MX).start()
+
+    @pl.loop(0, 4)
+    def _(trip):
+        for k in range(4):
+            one_pair(trip * 4 + k)
 
     for j in range(16):
         part_copy(out_ref, out_hbm, sems, j, 2 * MX).wait()
@@ -1020,7 +1029,8 @@
         scratch_shapes=[
             pltpu.VMEM(spectral_weight.shape, BF16),
             pltpu.VMEM((MX // 4, 128, 64), BF16),
-            pltpu.VMEM((2, 64, 128), F32),
+            pltpu.VMEM((16, 128, 64), BF16),
+            pltpu.VMEM((32, 64, 128), F32),
             sems(16),
         ],
         compiler_params=params(VMEM_MIB),

time: 94.1 us -> 90.1 us (0.957)
  local copies, waits for them, and re-layouts: 8.42 us -> 0.04 us
  waiting for transfers between devices: 5.93 us -> 11.7 us
  Pallas kernels: 50.5 us -> 49.2 us
    unnamed x20 -> x12, local copies, waits for them, and re-layouts: 8.42 us -> 0.04 us
    all_to_all x3, waiting for transfers between devices: 5.93 us -> 11.7 us  [exchange(): lax.all_to_all(block.reshape(devices, 64, 128), 'gx', 0, 0, tiled=True)]
    pallas_call x2, Pallas kernels: 10.8 us -> 9.55 us  [point(): pl.pallas_call(functools.partial(point_kernel, transposed), out_shape=[pl...]
  transfers between devices with their start and end apart: 3 -> 3, of which waited for: 3 -> 3; matrix products, arithmetic and copies ran while one was open for 0% -> 0% of each run, Pallas kernels for 21% -> 20%
where the time goes in v2:
time: 90.1 us; the launch traced here: 89.5 us
  Pallas kernels  49.2 us (55%)
  starting transfers between devices  14.7 us (16%)
  blocking collectives  12.8 us (14%)
  waiting for transfers between devices  11.7 us (13%)
  between operations  0.95 us (1%)
    all_to_all x3, starting transfers between devices, exchange(): lax.all_to_all(block.reshape(devices, 64, 128), 'gx', 0, 0, tiled=True)  14.7 us
    all_to_all x1, blocking collectives, exchange(): lax.all_to_all(block.reshape(devices, 64, 128), 'gx', 0, 0, tiled=True)  12.8 us
    all_to_all x3, waiting for transfers between devices, exchange(): lax.all_to_all(block.reshape(devices, 64, 128), 'gx', 0, 0, tiled=True)  11.7 us
    pallas_call x2, Pallas kernels, point(): pl.pallas_call(functools.partial(point_kernel, transposed), out_shape=[pl...  9.55 us
    pallas_call x1, Pallas kernels, fast_body(): pl.pallas_call(functools.partial(middle_kernel, inverse_scale), out_shape...  8.63 us
    pallas_call x1, Pallas kernels, fast_body(): pl.pallas_call(functools.partial(weight_grad_kernel, weight_scale), out_s...  8.45 us
    pallas_call x1, Pallas kernels, fast_body(): pl.pallas_call(functools.partial(mode_grad_kernel, forward_scale), out_sh...  8.32 us
    pallas_call x1, Pallas kernels, fast_body(): pl.pallas_call(functools.partial(mode_kernel, forward_scale), out_shape=[...  6.64 us
  transfers between devices with their start and end apart: 3, of which 3 were waited for; matrix products, arithmetic and copies ran while one was open for 0% of the time, Pallas kernels for 20%

profile of v2, /device:TPU:0, one launch (start us, length us, event | category | flops | bytes accessed | tf_op | source)
XLA Modules:
  0.0 89.5 jit_solution(5141254779771463592)
XLA Ops:
  0.6 0.0 copy-start.1
  0.6 3.8 %field_analysis.1 = bf16[1024,128]{1,0:T(8,128)(2,1)} custom-call(bf16[64,2,64,128]{3,2,1,0:T(8,128)(2,1)} %field_hbm.3, bf16[64,256]{1,0:T(8,128)(2,1)} %constant.17.clone.pair_hbm, bf16[128,256]{1,0:T(8,128)(2,1)} %constant.18.clone.across_hbm), custom_call_target="tpu_custom_call" | custom-call | flops 536870912 | bytes 2097152 | tf_op jit(solution)/shard_map/field_analysis/pallas_call | solution.py:915
  4.4 7.4 %all-to-all-start = ((bf16[16,64,128]{2,1,0:T(8,128)(2,1)}), bf16[16,64,128]{2,1,0:T(8,128)(2,1)S(1)}, u32[]{:S(2)}, u32[]{:S(2)}) async-start(bf16[16,64,128]{2,1,0:T(8,128)(2,1)} %bitcast), calls=%async_computation | async-start | bytes 524288 | tf_op jit(solution)/shard_map/all_to_all | solution.py:889
  11.8 0.0 copy-done.1
  11.8 0.0 copy-start
  11.8 0.0 copy-start.3
  11.8 0.0 copy-start.4
  11.9 4.8 %channel_map.1 = (bf16[64,2,64,128]{3,2,1,0:T(8,128)(2,1)}, bf16[8192,128]{1,0:T(8,128)(2,1)S(1)}) custom-call(bf16[64,64]{1,0:T(8,128)(2,1)S(1)} %copy-done.1, bf16[64,2,64,128]{3,2,1,0:T(8,128)(2,1)} %field_hbm.3, bf16[65536,128]{1,0:T(8,128)(2,1)} %bitcast.14), custom_call_target="tpu_custom_call" | custom-call | flops 2147483648 | bytes 4194304 | tf_op jit(solution)/shard_map/channel_map/pallas_call | solution.py:894
  16.6 5.2 %all-to-all-done = bf16[16,64,128]{2,1,0:T(8,128)(2,1)S(1)} async-done(((bf16[16,64,128]{2,1,0:T(8,128)(2,1)}), bf16[16,64,128]{2,1,0:T(8,128)(2,1)S(1)}, u32[]{:S(2)}, u32[]{:S(2)}) %all-to-all-start) | async-done | bytes 262176 | tf_op jit(solution)/shard_map/all_to_all | solution.py:889
  21.9 0.0 copy-done
  21.9 0.0 copy-done.3
  21.9 0.0 copy-done.4
  21.9 0.0 copy-start.5
  21.9 6.6 %mode_product.1 = (bf16[16,64,128]{2,1,0:T(8,128)(2,1)}, bf16[1024,128]{1,0:T(8,128)(2,1)S(1)}) custom-call(bf16[1024,128]{1,0:T(8,128)(2,1)S(1)} %bitcast.10, bf16[8192,128]{1,0:T(8,128)(2,1)S(1)} %get-tuple-element.24.head_ref, bf16[65536,128]{1,0:T(8,128)(2,1)} %bitcast.15, bf16[128,64]{1,0:T(8,128)(2,1)S(1)} %copy-done.3, bf16[64,64]{1,0:T(8,128)(2,1)S(1)} %copy-done.4, ...), custom_call_target="tpu_custom_call" | custom-call | flops 268435456 | bytes 17825792 | tf_op jit(solution)/shard_map/mode_product/pallas_call | solution.py:941
  28.5 12.8 %all_to_all.20 = bf16[16,64,128]{2,1,0:T(8,128)(2,1)S(1)} all-to-all(bf16[16,64,128]{2,1,0:T(8,128)(2,1)S(1)} %bitcast.13), channel_id=1, replica_groups=mesh['grp'=2,'gx'=16] {'gx'}, dimensions={0} | all-to-all | bytes 524288 | tf_op jit(solution)/shard_map/all_to_all | solution.py:889
  41.4 0.0 copy-done.5
  41.4 8.6 %gelu_and_gradient.1 = (bf16[64,2,64,128]{3,2,1,0:T(8,128)(2,1)}, bf16[64,2,64,128]{3,2,1,0:T(8,128)(2,1)}, bf16[1024,128]{1,0:T(8,128)(2,1)}) custom-call(bf16[1024,128]{1,0:T(8,128)(2,1)S(1)} %bitcast.12, f32[64]{0:T(128)S(1)} %copy-done.5, bf16[64,2,64,128]{3,2,1,0:T(8,128)(2,1)} %get-tuple-element.26.point_hbm, bf16[64,2,64,128]{3,2,1,0:T(8,128)(2,1)} %cot_hbm.1, ...), custom_call_target="tpu_custom_call" | custom-call | flops 1073741824 | bytes 8388608 | tf_op jit(solution)/shard_map/gelu_and_gradient/pallas_call | solution.py:962
  50.0 3.5 %all-to-all-start.2 = ((bf16[16,64,128]{2,1,0:T(8,128)(2,1)}), bf16[16,64,128]{2,1,0:T(8,128)(2,1)S(1)}, u32[]{:S(2)}, u32[]{:S(2)}) async-start(bf16[16,64,128]{2,1,0:T(8,128)(2,1)} %bitcast.5), calls=%async_computation.2 | async-start | bytes 524288 | tf_op jit(solution)/shard_map/all_to_all | solution.py:889
  53.5 0.0 copy-start.2
  53.6 4.8 %channel_map_back.1 = (bf16[64,2,64,128]{3,2,1,0:T(8,128)(2,1)}, bf16[8192,128]{1,0:T(8,128)(2,1)S(1)}) custom-call(bf16[64,64]{1,0:T(8,128)(2,1)S(1)} %copy-done.1, bf16[64,2,64,128]{3,2,1,0:T(8,128)(2,1)} %get-tuple-element.29.field_hbm, bf16[65536,128]{1,0:T(8,128)(2,1)} %bitcast.16), custom_call_target="tpu_custom_call" | custom-call | flops 2147483648 | bytes 4194304 | tf_op jit(solution)/shard_map/channel_map_back/pallas_call | solution.py:894
  58.3 5.2 %all-to-all-done.2 = bf16[16,64,128]{2,1,0:T(8,128)(2,1)S(1)} async-done(((bf16[16,64,128]{2,1,0:T(8,128)(2,1)}), bf16[16,64,128]{2,1,0:T(8,128)(2,1)S(1)}, u32[]{:S(2)}, u32[]{:S(2)}) %all-to-all-start.2) | async-done | bytes 262176 | tf_op jit(solution)/shard_map/all_to_all | solution.py:889
  63.5 0.0 copy-done.2
  63.6 8.3 %mode_gradient.1 = (bf16[32,64,128]{2,1,0:T(8,128)(2,1)S(1)}, bf16[16,64,128]{2,1,0:T(8,128)(2,1)S(1)}, bf16[1024,128]{1,0:T(8,128)(2,1)}) custom-call(bf16[1024,128]{1,0:T(8,128)(2,1)S(1)} %bitcast.9, bf16[8192,128]{1,0:T(8,128)(2,1)S(1)} %get-tuple-element.33.head_ref, bf16[65536,128]{1,0:T(8,128)(2,1)} %bitcast.17, bf16[128,64]{1,0:T(8,128)(2,1)S(1)} %copy-done.2, ...), custom_call_target="tpu_custom_call" | custom-call | flops 268435456 | bytes 17825792 | tf_op jit(solution)/shard_map/mode_gradient/pallas_call | solution.py:1001
  71.9 3.8 %all-to-all-start.3 = ((bf16[16,64,128]{2,1,0:T(8,128)(2,1)}), bf16[16,64,128]{2,1,0:T(8,128)(2,1)S(1)}, u32[]{:S(2)}, u32[]{:S(2)}) async-start(bf16[16,64,128]{2,1,0:T(8,128)(2,1)} %bitcast.7), calls=%async_computation.3 | async-start | bytes 524288 | tf_op jit(solution)/shard_map/all_to_all | solution.py:889
  75.7 8.5 %weight_gradient.1 = bf16[1024,64,128]{2,1,0:T(8,128)(2,1)} custom-call(bf16[16,64,128]{2,1,0:T(8,128)(2,1)S(1)} %get-tuple-element.37.coeff_ref, bf16[32,64,128]{2,1,0:T(8,128)(2,1)S(1)} %get-tuple-element.38.pair_ref), custom_call_target="tpu_custom_call" | custom-call | flops 1073741824 | bytes 17825792 | tf_op jit(solution)/shard_map/weight_gradient/pallas_call | solution.py:1024
  84.1 1.3 %all-to-all-done.3 = bf16[16,64,128]{2,1,0:T(8,128)(2,1)S(1)} async-done(((bf16[16,64,128]{2,1,0:T(8,128)(2,1)}), bf16[16,64,128]{2,1,0:T(8,128)(2,1)S(1)}, u32[]{:S(2)}, u32[]{:S(2)}) %all-to-all-start.3) | async-done | bytes 262176 | tf_op jit(solution)/shard_map/all_to_all | solution.py:889
  85.4 3.8 %field_gradient.1 = bf16[64,2,64,128]{3,2,1,0:T(8,128)(2,1)} custom-call(bf16[1024,128]{1,0:T(8,128)(2,1)S(1)} %bitcast.11, bf16[64,2,64,128]{3,2,1,0:T(8,128)(2,1)} %get-tuple-element.36.point_hbm, bf16[256,1024]{1,0:T(8,128)(2,1)} %constant.16.clone.depth_hbm, bf16[256,128]{1,0:T(8,128)(2,1)} %constant.19.clone.back_hbm), custom_call_target="tpu_custom_call" | custom-call | flops 536870912 | bytes 4194304 | tf_op jit(solution)/shard_map/field_gradient/pallas_call | solution.py:1044
Async XLA Ops:
  0.6 11.2 %copy-start.1 = (bf16[64,64]{1,0:T(8,128)(2,1)S(1)}, bf16[64,64]{1,0:T(8,128)(2,1)}, u32[]{:S(2)}) copy-start(bf16[64,64]{1,0:T(8,128)(2,1)} %weight_ref.3) | copy-start | bytes 24580
  4.4 17.4 %all-to-all-start = ((bf16[16,64,128]{2,1,0:T(8,128)(2,1)}), bf16[16,64,128]{2,1,0:T(8,128)(2,1)S(1)}, u32[]{:S(2)}, u32[]{:S(2)}) async-start(bf16[16,64,128]{2,1,0:T(8,128)(2,1)} %bitcast), calls=%async_computation | async-start | bytes 524288 | tf_op jit(solution)/shard_map/all_to_all | solution.py:889
  11.8 10.0 %copy-start = (bf16[64,64]{1,0:T(8,128)(2,1)S(1)}, bf16[64,64]{1,0:T(8,128)(2,1)}, u32[]{:S(2)}) copy-start(bf16[64,64]{1,0:T(8,128)(2,1)} %constant.23.clone.back_ref) | copy-start | bytes 24580
  11.8 10.0 %copy-start.3 = (bf16[128,64]{1,0:T(8,128)(2,1)S(1)}, bf16[128,64]{1,0:T(8,128)(2,1)}, u32[]{:S(2)}) copy-start(bf16[128,64]{1,0:T(8,128)(2,1)} %constant.21.clone.both_ref) | copy-start | bytes 49156
  11.8 10.0 %copy-start.4 = (bf16[64,64]{1,0:T(8,128)(2,1)S(1)}, bf16[64,64]{1,0:T(8,128)(2,1)}, u32[]{:S(2)}) copy-start(bf16[64,64]{1,0:T(8,128)(2,1)} %constant.20.clone.plain_ref) | copy-start | bytes 24580
  21.9 19.5 %copy-start.5 = (f32[64]{0:T(128)S(1)}, f32[64]{0:T(128)}, u32[]{:S(2)}) copy-start(f32[64]{0:T(128)} %bias_ref.1) | copy-start | bytes 772
  50.0 13.6 %all-to-all-start.2 = ((bf16[16,64,128]{2,1,0:T(8,128)(2,1)}), bf16[16,64,128]{2,1,0:T(8,128)(2,1)S(1)}, u32[]{:S(2)}, u32[]{:S(2)}) async-start(bf16[16,64,128]{2,1,0:T(8,128)(2,1)} %bitcast.5), calls=%async_computation.2 | async-start | bytes 524288 | tf_op jit(solution)/shard_map/all_to_all | solution.py:889
  53.5 10.0 %copy-start.2 = (bf16[128,64]{1,0:T(8,128)(2,1)S(1)}, bf16[128,64]{1,0:T(8,128)(2,1)}, u32[]{:S(2)}) copy-start(bf16[128,64]{1,0:T(8,128)(2,1)} %constant.22.clone.straight_ref) | copy-start | bytes 49156
  71.9 13.6 %all-to-all-start.3 = ((bf16[16,64,128]{2,1,0:T(8,128)(2,1)}), bf16[16,64,128]{2,1,0:T(8,128)(2,1)S(1)}, u32[]{:S(2)}, u32[]{:S(2)}) async-start(bf16[16,64,128]{2,1,0:T(8,128)(2,1)} %bitcast.7), calls=%async_computation.3 | async-start | bytes 524288 | tf_op jit(solution)/shard_map/all_to_all | solution.py:889

commit v3 on v2

--- a/solution.py
+++ b/solution.py
@@ -201,7 +201,7 @@
 VMEM_MIB = 32
 VECTOR = 2
 HEAD = 2
-WAITS = {2: 2, 4: 4, 8: 4, 12: 4}
+FLIGHT = 6
 NT = (((1,), (1,)), ((), ()))
 F32 = jnp.float32
 BF16 = jnp.bfloat16
@@ -286,8 +286,8 @@
     return pltpu.make_async_copy(source.at[part], target.at[part], sems.at[index])
 
 
-def start_parts(source, target, sems, size):
-    for index in range(source.shape[0] // size):
+def start_parts(source, target, sems, size, first, last):
+    for index in range(first, min(last, source.shape[0] // size)):
         part_copy(source, target, sems, index, size).start()
 
 
@@ -405,11 +405,12 @@
     table_sems,
 ):
     first, second = start_tables([(pair_hbm, pair_ref), (across_hbm, across_ref)], table_sems)
-    start_parts(field_hbm, field_ref, field_sems, STEP)
+    start_parts(field_hbm, field_ref, field_sems, STEP, 0, 2)
     first.wait()
 
     for step in range(field_ref.shape[0] // STEP):
         part_copy(field_hbm, field_ref, field_sems, step, STEP).wait()
+        start_parts(field_hbm, field_ref, field_sems, STEP, step + 2, step + 3)
         for g in range(STEP // GROUP):
             group = step * (STEP // GROUP) + g
             slabs = [flat(field_ref[group * GROUP + ci]) for ci in range(GROUP)]
@@ -458,9 +459,11 @@
         ],
         table_sems,
     )
-    start_parts(point_hbm, point_ref, point_sems, STEP)
-    start_parts(cot_hbm, cot_ref, cot_sems, STEP)
+    start_parts(point_hbm, point_ref, point_sems, STEP, 0, 1)
+    start_parts(cot_hbm, cot_ref, cot_sems, STEP, 0, 1)
     rows_gather(block_ref, rows_ref, spec_ref)
+    start_parts(point_hbm, point_ref, point_sems, STEP, 1, 2)
+    start_parts(cot_hbm, cot_ref, cot_sems, STEP, 1, 2)
     for copy in tables_in:
         copy.wait()
     steps = point_ref.shape[0] // STEP
@@ -489,6 +492,8 @@
         if group % per_step == 0:
             part_copy(point_hbm, point_ref, point_sems, step, STEP).wait()
             part_copy(cot_hbm, cot_ref, cot_sems, step, STEP).wait()
+            start_parts(point_hbm, point_ref, point_sems, STEP, step + 2, step + 3)
+            start_parts(cot_hbm, cot_ref, cot_sems, STEP, step + 2, step + 3)
             if step + 1 < steps:
                 wides += lines_synthesis(step + 1, spec_ref, back_ref[...], inverse_scale)
         following, slabs = [], []
@@ -530,8 +535,9 @@
     table_sems,
 ):
     tables_in = start_tables([(back_hbm, back_ref), (depth_hbm, depth_ref)], table_sems)
-    start_parts(point_hbm, point_ref, point_sems, STEP)
+    start_parts(point_hbm, point_ref, point_sems, STEP, 0, 1)
     rows_gather(block_ref, rows_ref, spec_ref)
+    start_parts(point_hbm, point_ref, point_sems, STEP, 1, 4)
     for copy in tables_in:
         copy.wait()
     steps = point_ref.shape[0] // STEP
@@ -587,7 +593,9 @@
         copy = pltpu.make_async_copy(field_hbm.at[part], field_ref.at[part], in_sems.at[plane])
         copy.start()
         copies.append(copy)
-    heads = start_weights(modes_hbm, head_ref, head_sems, 0)
+    heads = weight_copies(modes_hbm, head_ref, head_sems, 0)
+    for copy in heads:
+        copy.start()
     tall = (sublanes((size, 64)) // 16 == lanes((size, 64))).astype(BF16)
     weight = weight_ref[...]
     left = dot_nt(tall, weight) if transposed else dot_nn(tall, weight)
@@ -624,7 +632,7 @@
         copy.wait()
 
 
-def start_weights(weight_hbm, weight_ref, sems, first):
+def weight_copies(weight_hbm, weight_ref, sems, first):
     rows = weight_hbm.shape[0] // 16
     copies = []
     for index in range(weight_ref.shape[0] // rows):
@@ -633,9 +641,17 @@
             weight_ref.at[pl.ds(index * rows, rows)],
             sems.at[index],
         )
-        copy.start()
         copies.append(copy)
     return copies
+
+
+def next_weights(copies, j):
+    if j < HEAD or j % 2:
+        return
+    for index in (j - HEAD, j - HEAD + 1):
+        copies[index].wait()
+        if index + FLIGHT < len(copies):
+            copies[index + FLIGHT].start()
 
 
 def mode_pair(head_ref, weight_ref, j, h, u):
@@ -673,7 +689,9 @@
     sems,
     coeff_sems,
 ):
-    copies = start_weights(weight_hbm, weight_ref, sems, HEAD)
+    copies = weight_copies(weight_hbm, weight_ref, sems, HEAD)
+    for copy in copies[:FLIGHT]:
+        copy.start()
     count = rows_ref.shape[0] // 16
     rows_ref[...] = block_ref[...].astype(F32)
     low = lanes((128, 128)) < 64
@@ -700,8 +718,7 @@
     send = pltpu.make_async_copy(coeff_ref, coeff_hbm, coeff_sems.at[0])
     send.start()
     for j in range(16):
-        for copy in copies[j - HEAD : j - HEAD + WAITS.get(j, 0)]:
-            copy.wait()
+        next_weights(copies, j)
         mixed = []
         for u in range(MX // 8):
             halves = [
@@ -716,8 +733,9 @@
                 move = jnp.where(low8, high_h[:8], sign * low_h[8:])
                 mixed.append(keep + swap_halves(move))
         mixed_ref[j] = jnp.concatenate(mixed, axis=0).astype(BF16)
-        if j % 4 == 3:
-            plane_sums(back_ref, mixed_ref, res_ref, j // 4)
+        if j > 4 and j % 4 == 1:
+            plane_sums(back_ref, mixed_ref, res_ref, j // 4 - 1)
+    plane_sums(back_ref, mixed_ref, res_ref, 3)
     out_ref[...] = res_ref[...].astype(BF16)
     send.wait()
 
@@ -742,7 +760,9 @@
 ):
     send = pltpu.make_async_copy(coeff_hbm, coeff_ref, coeff_sems.at[0])
     send.start()
-    copies = start_weights(weight_hbm, weight_ref, sems, HEAD)
+    copies = weight_copies(weight_hbm, weight_ref, sems, HEAD)
+    for copy in copies[:FLIGHT]:
+        copy.start()
     count = rows_ref.shape[0] // 16
     rows_ref[...] = block_ref[...].astype(F32)
     low = lanes((64, 128)) < 64
@@ -763,8 +783,7 @@
             part = turned[:, h * 128 : (h + 1) * 128]
             pair_ref[2 * j + h] = jnp.where(low, part[:64], part[64:]).astype(BF16)
     for j in range(16):
-        for copy in copies[j - HEAD : j - HEAD + WAITS.get(j, 0)]:
-            copy.wait()
+        next_weights(copies, j)
         mixed = []
         for u in range(MX // 8):
             found = []
@@ -779,8 +798,9 @@
             move = jnp.where(low16, found[1], found[0])
             mixed.append(keep + swap_halves(move))
         mixed_ref[j] = (jnp.concatenate(mixed, axis=0) * scale).astype(BF16)
-    for quarter in range(4):
-        plane_sums(back_ref, mixed_ref, res_ref, quarter)
+        if j > 4 and j % 4 == 1:
+            plane_sums(back_ref, mixed_ref, res_ref, j // 4 - 1)
+    plane_sums(back_ref, mixed_ref, res_ref, 3)
     out_ref[...] = res_ref[...].astype(BF16)
     send.wait()
 

time: 90.1 us -> 89.8 us (level)
  no operation moved by 1% of the time
where the time goes in v3:
time: 89.8 us; the launch traced here: 89.2 us
  Pallas kernels  49 us (55%)
  starting transfers between devices  14.7 us (16%)
  blocking collectives  12.8 us (14%)
  waiting for transfers between devices  11.7 us (13%)
  between operations  0.95 us (1%)
    all_to_all x3, starting transfers between devices, exchange(): lax.all_to_all(block.reshape(devices, 64, 128), 'gx', 0, 0, tiled=True)  14.7 us
    all_to_all x1, blocking collectives, exchange(): lax.all_to_all(block.reshape(devices, 64, 128), 'gx', 0, 0, tiled=True)  12.8 us
    all_to_all x3, waiting for transfers between devices, exchange(): lax.all_to_all(block.reshape(devices, 64, 128), 'gx', 0, 0, tiled=True)  11.7 us
    pallas_call x2, Pallas kernels, point(): pl.pallas_call(functools.partial(point_kernel, transposed), out_shape=[pl...  9.55 us
    pallas_call x1, Pallas kernels, fast_body(): pl.pallas_call(functools.partial(weight_grad_kernel, weight_scale), out_s...  8.46 us
    pallas_call x1, Pallas kernels, fast_body(): pl.pallas_call(functools.partial(middle_kernel, inverse_scale), out_shape...  8.35 us
    pallas_call x1, Pallas kernels, fast_body(): pl.pallas_call(functools.partial(mode_grad_kernel, forward_scale), out_sh...  8.17 us
    pallas_call x1, Pallas kernels, fast_body(): pl.pallas_call(functools.partial(mode_kernel, forward_scale), out_shape=[...  6.38 us
  transfers between devices with their start and end apart: 3, of which 3 were waited for; matrix products, arithmetic and copies ran while one was open for 0% of the time, Pallas kernels for 20%

profile of v3, /device:TPU:0, one launch (start us, length us, event | category | flops | bytes accessed | tf_op | source)
XLA Modules:
  0.0 89.2 jit_solution(3740352977765174501)
XLA Ops:
  0.6 0.0 copy-start.1
  0.6 4.2 %field_analysis.1 = bf16[1024,128]{1,0:T(8,128)(2,1)} custom-call(bf16[64,2,64,128]{3,2,1,0:T(8,128)(2,1)} %field_hbm.3, bf16[64,256]{1,0:T(8,128)(2,1)} %constant.17.clone.pair_hbm, bf16[128,256]{1,0:T(8,128)(2,1)} %constant.18.clone.across_hbm), custom_call_target="tpu_custom_call" | custom-call | flops 536870912 | bytes 2097152 | tf_op jit(solution)/shard_map/field_analysis/pallas_call | solution.py:935
  4.9 7.4 %all-to-all-start = ((bf16[16,64,128]{2,1,0:T(8,128)(2,1)}), bf16[16,64,128]{2,1,0:T(8,128)(2,1)S(1)}, u32[]{:S(2)}, u32[]{:S(2)}) async-start(bf16[16,64,128]{2,1,0:T(8,128)(2,1)} %bitcast), calls=%async_computation | async-start | bytes 524288 | tf_op jit(solution)/shard_map/all_to_all | solution.py:909
  12.3 0.0 copy-done.1
  12.3 0.0 copy-start
  12.3 0.0 copy-start.3
  12.3 0.0 copy-start.4
  12.3 4.8 %channel_map.1 = (bf16[64,2,64,128]{3,2,1,0:T(8,128)(2,1)}, bf16[8192,128]{1,0:T(8,128)(2,1)S(1)}) custom-call(bf16[64,64]{1,0:T(8,128)(2,1)S(1)} %copy-done.1, bf16[64,2,64,128]{3,2,1,0:T(8,128)(2,1)} %field_hbm.3, bf16[65536,128]{1,0:T(8,128)(2,1)} %bitcast.14), custom_call_target="tpu_custom_call" | custom-call | flops 2147483648 | bytes 4194304 | tf_op jit(solution)/shard_map/channel_map/pallas_call | solution.py:914
  17.1 5.2 %all-to-all-done = bf16[16,64,128]{2,1,0:T(8,128)(2,1)S(1)} async-done(((bf16[16,64,128]{2,1,0:T(8,128)(2,1)}), bf16[16,64,128]{2,1,0:T(8,128)(2,1)S(1)}, u32[]{:S(2)}, u32[]{:S(2)}) %all-to-all-start) | async-done | bytes 262176 | tf_op jit(solution)/shard_map/all_to_all | solution.py:909
  22.3 0.0 copy-done
  22.3 0.0 copy-done.3
  22.3 0.0 copy-done.4
  22.3 0.0 copy-start.5
  22.3 6.4 %mode_product.1 = (bf16[16,64,128]{2,1,0:T(8,128)(2,1)}, bf16[1024,128]{1,0:T(8,128)(2,1)S(1)}) custom-call(bf16[1024,128]{1,0:T(8,128)(2,1)S(1)} %bitcast.10, bf16[8192,128]{1,0:T(8,128)(2,1)S(1)} %get-tuple-element.24.head_ref, bf16[65536,128]{1,0:T(8,128)(2,1)} %bitcast.15, bf16[128,64]{1,0:T(8,128)(2,1)S(1)} %copy-done.3, bf16[64,64]{1,0:T(8,128)(2,1)S(1)} %copy-done.4, ...), custom_call_target="tpu_custom_call" | custom-call | flops 268435456 | bytes 17825792 | tf_op jit(solution)/shard_map/mode_product/pallas_call | solution.py:961
  28.7 12.8 %all_to_all.20 = bf16[16,64,128]{2,1,0:T(8,128)(2,1)S(1)} all-to-all(bf16[16,64,128]{2,1,0:T(8,128)(2,1)S(1)} %bitcast.13), channel_id=1, replica_groups=mesh['grp'=2,'gx'=16] {'gx'}, dimensions={0} | all-to-all | bytes 524288 | tf_op jit(solution)/shard_map/all_to_all | solution.py:909
  41.6 0.0 copy-done.5
  41.6 8.3 %gelu_and_gradient.1 = (bf16[64,2,64,128]{3,2,1,0:T(8,128)(2,1)}, bf16[64,2,64,128]{3,2,1,0:T(8,128)(2,1)}, bf16[1024,128]{1,0:T(8,128)(2,1)}) custom-call(bf16[1024,128]{1,0:T(8,128)(2,1)S(1)} %bitcast.12, f32[64]{0:T(128)S(1)} %copy-done.5, bf16[64,2,64,128]{3,2,1,0:T(8,128)(2,1)} %get-tuple-element.26.point_hbm, bf16[64,2,64,128]{3,2,1,0:T(8,128)(2,1)} %cot_hbm.1, ...), custom_call_target="tpu_custom_call" | custom-call | flops 1073741824 | bytes 8388608 | tf_op jit(solution)/shard_map/gelu_and_gradient/pallas_call | solution.py:982
  49.9 3.5 %all-to-all-start.2 = ((bf16[16,64,128]{2,1,0:T(8,128)(2,1)}), bf16[16,64,128]{2,1,0:T(8,128)(2,1)S(1)}, u32[]{:S(2)}, u32[]{:S(2)}) async-start(bf16[16,64,128]{2,1,0:T(8,128)(2,1)} %bitcast.5), calls=%async_computation.2 | async-start | bytes 524288 | tf_op jit(solution)/shard_map/all_to_all | solution.py:909
  53.5 0.0 copy-start.2
  53.5 4.8 %channel_map_back.1 = (bf16[64,2,64,128]{3,2,1,0:T(8,128)(2,1)}, bf16[8192,128]{1,0:T(8,128)(2,1)S(1)}) custom-call(bf16[64,64]{1,0:T(8,128)(2,1)S(1)} %copy-done.1, bf16[64,2,64,128]{3,2,1,0:T(8,128)(2,1)} %get-tuple-element.29.field_hbm, bf16[65536,128]{1,0:T(8,128)(2,1)} %bitcast.16), custom_call_target="tpu_custom_call" | custom-call | flops 2147483648 | bytes 4194304 | tf_op jit(solution)/shard_map/channel_map_back/pallas_call | solution.py:914
  58.3 5.2 %all-to-all-done.2 = bf16[16,64,128]{2,1,0:T(8,128)(2,1)S(1)} async-done(((bf16[16,64,128]{2,1,0:T(8,128)(2,1)}), bf16[16,64,128]{2,1,0:T(8,128)(2,1)S(1)}, u32[]{:S(2)}, u32[]{:S(2)}) %all-to-all-start.2) | async-done | bytes 262176 | tf_op jit(solution)/shard_map/all_to_all | solution.py:909
  63.5 0.0 copy-done.2
  63.5 8.2 %mode_gradient.1 = (bf16[32,64,128]{2,1,0:T(8,128)(2,1)S(1)}, bf16[16,64,128]{2,1,0:T(8,128)(2,1)S(1)}, bf16[1024,128]{1,0:T(8,128)(2,1)}) custom-call(bf16[1024,128]{1,0:T(8,128)(2,1)S(1)} %bitcast.9, bf16[8192,128]{1,0:T(8,128)(2,1)S(1)} %get-tuple-element.33.head_ref, bf16[65536,128]{1,0:T(8,128)(2,1)} %bitcast.17, bf16[128,64]{1,0:T(8,128)(2,1)S(1)} %copy-done.2, ...), custom_call_target="tpu_custom_call" | custom-call | flops 268435456 | bytes 17825792 | tf_op jit(solution)/shard_map/mode_gradient/pallas_call | solution.py:1021
  71.6 3.8 %all-to-all-start.3 = ((bf16[16,64,128]{2,1,0:T(8,128)(2,1)}), bf16[16,64,128]{2,1,0:T(8,128)(2,1)S(1)}, u32[]{:S(2)}, u32[]{:S(2)}) async-start(bf16[16,64,128]{2,1,0:T(8,128)(2,1)} %bitcast.7), calls=%async_computation.3 | async-start | bytes 524288 | tf_op jit(solution)/shard_map/all_to_all | solution.py:909
  75.4 8.5 %weight_gradient.1 = bf16[1024,64,128]{2,1,0:T(8,128)(2,1)} custom-call(bf16[16,64,128]{2,1,0:T(8,128)(2,1)S(1)} %get-tuple-element.37.coeff_ref, bf16[32,64,128]{2,1,0:T(8,128)(2,1)S(1)} %get-tuple-element.38.pair_ref), custom_call_target="tpu_custom_call" | custom-call | flops 1073741824 | bytes 17825792 | tf_op jit(solution)/shard_map/weight_gradient/pallas_call | solution.py:1044
  83.9 1.3 %all-to-all-done.3 = bf16[16,64,128]{2,1,0:T(8,128)(2,1)S(1)} async-done(((bf16[16,64,128]{2,1,0:T(8,128)(2,1)}), bf16[16,64,128]{2,1,0:T(8,128)(2,1)S(1)}, u32[]{:S(2)}, u32[]{:S(2)}) %all-to-all-start.3) | async-done | bytes 262176 | tf_op jit(solution)/shard_map/all_to_all | solution.py:909
  85.2 3.9 %field_gradient.1 = bf16[64,2,64,128]{3,2,1,0:T(8,128)(2,1)} custom-call(bf16[1024,128]{1,0:T(8,128)(2,1)S(1)} %bitcast.11, bf16[64,2,64,128]{3,2,1,0:T(8,128)(2,1)} %get-tuple-element.36.point_hbm, bf16[256,1024]{1,0:T(8,128)(2,1)} %constant.16.clone.depth_hbm, bf16[256,128]{1,0:T(8,128)(2,1)} %constant.19.clone.back_hbm), custom_call_target="tpu_custom_call" | custom-call | flops 536870912 | bytes 4194304 | tf_op jit(solution)/shard_map/field_gradient/pallas_call | solution.py:1064
Async XLA Ops:
  0.6 11.6 %copy-start.1 = (bf16[64,64]{1,0:T(8,128)(2,1)S(1)}, bf16[64,64]{1,0:T(8,128)(2,1)}, u32[]{:S(2)}) copy-start(bf16[64,64]{1,0:T(8,128)(2,1)} %weight_ref.3) | copy-start | bytes 24580
  4.9 17.4 %all-to-all-start = ((bf16[16,64,128]{2,1,0:T(8,128)(2,1)}), bf16[16,64,128]{2,1,0:T(8,128)(2,1)S(1)}, u32[]{:S(2)}, u32[]{:S(2)}) async-start(bf16[16,64,128]{2,1,0:T(8,128)(2,1)} %bitcast), calls=%async_computation | async-start | bytes 524288 | tf_op jit(solution)/shard_map/all_to_all | solution.py:909
  12.3 10.0 %copy-start = (bf16[64,64]{1,0:T(8,128)(2,1)S(1)}, bf16[64,64]{1,0:T(8,128)(2,1)}, u32[]{:S(2)}) copy-start(bf16[64,64]{1,0:T(8,128)(2,1)} %constant.23.clone.back_ref) | copy-start | bytes 24580
  12.3 10.0 %copy-start.3 = (bf16[128,64]{1,0:T(8,128)(2,1)S(1)}, bf16[128,64]{1,0:T(8,128)(2,1)}, u32[]{:S(2)}) copy-start(bf16[128,64]{1,0:T(8,128)(2,1)} %constant.21.clone.both_ref) | copy-start | bytes 49156
  12.3 10.0 %copy-start.4 = (bf16[64,64]{1,0:T(8,128)(2,1)S(1)}, bf16[64,64]{1,0:T(8,128)(2,1)}, u32[]{:S(2)}) copy-start(bf16[64,64]{1,0:T(8,128)(2,1)} %constant.20.clone.plain_ref) | copy-start | bytes 24580
  22.3 19.2 %copy-start.5 = (f32[64]{0:T(128)S(1)}, f32[64]{0:T(128)}, u32[]{:S(2)}) copy-start(f32[64]{0:T(128)} %bias_ref.1) | copy-start | bytes 772
  49.9 13.6 %all-to-all-start.2 = ((bf16[16,64,128]{2,1,0:T(8,128)(2,1)}), bf16[16,64,128]{2,1,0:T(8,128)(2,1)S(1)}, u32[]{:S(2)}, u32[]{:S(2)}) async-start(bf16[16,64,128]{2,1,0:T(8,128)(2,1)} %bitcast.5), calls=%async_computation.2 | async-start | bytes 524288 | tf_op jit(solution)/shard_map/all_to_all | solution.py:909
  53.5 10.0 %copy-start.2 = (bf16[128,64]{1,0:T(8,128)(2,1)S(1)}, bf16[128,64]{1,0:T(8,128)(2,1)}, u32[]{:S(2)}) copy-start(bf16[128,64]{1,0:T(8,128)(2,1)} %constant.22.clone.straight_ref) | copy-start | bytes 49156
  71.6 13.6 %all-to-all-start.3 = ((bf16[16,64,128]{2,1,0:T(8,128)(2,1)}), bf16[16,64,128]{2,1,0:T(8,128)(2,1)S(1)}, u32[]{:S(2)}, u32[]{:S(2)}) async-start(bf16[16,64,128]{2,1,0:T(8,128)(2,1)} %bitcast.7), calls=%async_computation.3 | async-start | bytes 524288 | tf_op jit(solution)/shard_map/all_to_all | solution.py:909

commit v4 on v3

--- a/solution.py
+++ b/solution.py
@@ -199,8 +199,8 @@
 GROUP = 8
 STEP = 16
 VMEM_MIB = 32
-VECTOR = 2
-HEAD = 2
+VECTOR = 3
+HEAD = 3
 FLIGHT = 6
 NT = (((1,), (1,)), ((), ()))
 F32 = jnp.float32
@@ -405,12 +405,11 @@
     table_sems,
 ):
     first, second = start_tables([(pair_hbm, pair_ref), (across_hbm, across_ref)], table_sems)
-    start_parts(field_hbm, field_ref, field_sems, STEP, 0, 2)
+    start_parts(field_hbm, field_ref, field_sems, STEP, 0, field_ref.shape[0] // STEP)
     first.wait()
 
     for step in range(field_ref.shape[0] // STEP):
         part_copy(field_hbm, field_ref, field_sems, step, STEP).wait()
-        start_parts(field_hbm, field_ref, field_sems, STEP, step + 2, step + 3)
         for g in range(STEP // GROUP):
             group = step * (STEP // GROUP) + g
             slabs = [flat(field_ref[group * GROUP + ci]) for ci in range(GROUP)]
@@ -569,6 +568,30 @@
 
     for step in range(steps):
         part_copy(out_ref, out_hbm, out_sems, step, STEP).wait()
+
+
+def point_turn_kernel(
+    scale,
+    weight_ref,
+    field_hbm,
+    modes_hbm,
+    coeff_hbm,
+    out_hbm,
+    head_ref,
+    turned_hbm,
+    *refs,
+):
+    refs, (coeff_ref, turned_ref, turn_sems) = refs[:-3], refs[-3:]
+    take = pltpu.make_async_copy(coeff_hbm, coeff_ref, turn_sems.at[0])
+    take.start()
+    point_kernel(True, weight_ref, field_hbm, modes_hbm, out_hbm, head_ref, *refs)
+    take.wait()
+    eye = (sublanes((128, 128)) == lanes((128, 128))).astype(BF16)
+    for j in range(16):
+        turned_ref[j] = (dot_nt(eye, coeff_ref[j]) * scale).astype(BF16)
+    give = pltpu.make_async_copy(turned_ref, turned_hbm, turn_sems.at[1])
+    give.start()
+    give.wait()
 
 
 def point_kernel(
@@ -646,9 +669,9 @@
 
 
 def next_weights(copies, j):
-    if j < HEAD or j % 2:
+    if j < HEAD or (j - HEAD) % 2:
         return
-    for index in (j - HEAD, j - HEAD + 1):
+    for index in range(j - HEAD, min(j - HEAD + 2, len(copies))):
         copies[index].wait()
         if index + FLIGHT < len(copies):
             copies[index + FLIGHT].start()
@@ -747,22 +770,22 @@
     weight_hbm,
     straight_ref,
     back_ref,
-    coeff_hbm,
+    turned_hbm,
     pair_ref,
-    coeff_ref,
+    turned_ref,
     out_ref,
     weight_ref,
     rows_ref,
     res_ref,
     mixed_ref,
     sems,
-    coeff_sems,
+    turned_sems,
 ):
-    send = pltpu.make_async_copy(coeff_hbm, coeff_ref, coeff_sems.at[0])
-    send.start()
+    send = pltpu.make_async_copy(turned_hbm, turned_ref, turned_sems.at[0])
     copies = weight_copies(weight_hbm, weight_ref, sems, HEAD)
     for copy in copies[:FLIGHT]:
         copy.start()
+    send.start()
     count = rows_ref.shape[0] // 16
     rows_ref[...] = block_ref[...].astype(F32)
     low = lanes((64, 128)) < 64
@@ -806,17 +829,14 @@
 
 
 def weight_grad_kernel(
-    scale, coeff_ref, pair_ref, out_hbm, out_ref, mask_ref, turned_ref, pairs_ref, sems
+    turned_ref, pair_ref, out_hbm, out_ref, mask_ref, pairs_ref, sems
 ):
     lane = lanes((128, 64))
     part = sublanes((128, 64)) // 64
     for t in range(MX // 4 - VECTOR):
         mask_ref[t] = ((lane // 8 == t) & (lane % 4 // 2 == part)).astype(BF16)
-    eye = (sublanes((128, 128)) == lanes((128, 128))).astype(BF16)
-    for j in range(16):
-        turned_ref[j] = (dot_nt(eye, coeff_ref[j]) * scale).astype(BF16)
-        for h in range(2):
-            pairs_ref[2 * j + h] = pair_ref[2 * j + h].astype(F32)
+    for index in range(32):
+        pairs_ref[index] = pair_ref[index].astype(F32)
     even = (sublanes((64, 128)) % 2 == 0).astype(BF16)
     odd = (sublanes((64, 128)) % 2 == 1).astype(BF16)
 
@@ -910,27 +930,19 @@
             block.reshape(devices, 64, 128), "gx", 0, 0, tiled=True
         ).reshape(block_rows, 128)
 
-    def point(field, transposed):
-        return pl.pallas_call(
-            functools.partial(point_kernel, transposed),
-            out_shape=[
-                pltpu.HBM(features.shape, BF16),
-                pltpu.VMEM((weight_rows.shape[0] * HEAD // 16, weight_rows.shape[1]), BF16),
-            ],
-            in_specs=[vmem, hbm, hbm],
-            out_specs=[hbm, vmem],
-            scratch_shapes=[
-                field_scratch,
-                field_scratch,
-                pltpu.VMEM((channels * 16, channels * 16), BF16),
-                sems(planes),
-                sems(planes),
-                sems(HEAD),
-            ],
-            compiler_params=params(VMEM_MIB),
-            cost_estimate=cost(2 * 1024**3, 2 * field_bytes),
-            name="channel_map_back" if transposed else "channel_map",
-        )(channel_weight, in_hbm(field), weight_rows)
+    point_scratch = [
+        field_scratch,
+        field_scratch,
+        pltpu.VMEM((channels * 16, channels * 16), BF16),
+        sems(planes),
+        sems(planes),
+        sems(HEAD),
+    ]
+    point_out = [
+        pltpu.HBM(features.shape, BF16),
+        pltpu.VMEM((weight_rows.shape[0] * HEAD // 16, weight_rows.shape[1]), BF16),
+    ]
+    turned_shape = (16, 2 * channels, 64)
 
     block = pl.pallas_call(
         analysis_kernel,
@@ -950,7 +962,16 @@
         cost_estimate=cost(2 * 256 * 1024 * 1024, field_bytes),
         name="field_analysis",
     )(in_hbm(features), table["depth_pair"], table["across_y"])
-    pointwise, head = point(features, False)
+    pointwise, head = pl.pallas_call(
+        functools.partial(point_kernel, False),
+        out_shape=point_out,
+        in_specs=[vmem, hbm, hbm],
+        out_specs=[hbm, vmem],
+        scratch_shapes=point_scratch,
+        compiler_params=params(VMEM_MIB),
+        cost_estimate=cost(2 * 1024**3, 2 * field_bytes),
+        name="channel_map",
+    )(channel_weight, in_hbm(features), weight_rows)
     block, pointwise, head = lax.optimization_barrier((exchange(block), pointwise, head))
 
     weight_scratch = pltpu.VMEM(
@@ -1015,14 +1036,26 @@
         table["across_y"],
         table["back_y"],
     )
-    channel_back, head = point(upstream, True)
-    block, channel_back, head = lax.optimization_barrier((exchange(block), channel_back, head))
-
-    pairs, coeffs, block = pl.pallas_call(
+    channel_back, head, turned = pl.pallas_call(
+        functools.partial(point_turn_kernel, weight_scale),
+        out_shape=point_out + [pltpu.HBM(turned_shape, BF16)],
+        in_specs=[vmem, hbm, hbm, hbm],
+        out_specs=[hbm, vmem, hbm],
+        scratch_shapes=point_scratch
+        + [pltpu.VMEM((16, 64, 128), BF16), pltpu.VMEM(turned_shape, BF16), sems(2)],
+        compiler_params=params(VMEM_MIB),
+        cost_estimate=cost(2 * 1024**3, 2 * field_bytes),
+        name="channel_map_back",
+    )(channel_weight, in_hbm(upstream), weight_rows, in_hbm(coeffs))
+    block, channel_back, head, turned = lax.optimization_barrier(
+        (exchange(block), channel_back, head, turned)
+    )
+
+    pairs, turned, block = pl.pallas_call(
         functools.partial(mode_grad_kernel, forward_scale),
         out_shape=[
             pltpu.VMEM((32, 64, 128), BF16),
-            pltpu.VMEM((16, 64, 128), BF16),
+            pltpu.VMEM(turned_shape, BF16),
             block_shape,
         ],
         in_specs=[vmem, vmem, hbm, vmem, vmem, hbm],
@@ -1038,18 +1071,17 @@
         compiler_params=params(VMEM_MIB),
         cost_estimate=cost(256 * 2 * 16 * 256 * 128, 17 * 2**20),
         name="mode_gradient",
-    )(block, in_vmem(head), weight_rows, table["straight_x"], table["back_x"], in_hbm(coeffs))
+    )(block, in_vmem(head), weight_rows, table["straight_x"], table["back_x"], in_hbm(turned))
     block = exchange(block)
 
     spectral_grad = pl.pallas_call(
-        functools.partial(weight_grad_kernel, weight_scale),
+        weight_grad_kernel,
         out_shape=jax.ShapeDtypeStruct(spectral_weight.shape, BF16),
         in_specs=[vmem, vmem],
         out_specs=hbm,
         scratch_shapes=[
             pltpu.VMEM(spectral_weight.shape, BF16),
             pltpu.VMEM((MX // 4, 128, 64), BF16),
-            pltpu.VMEM((16, 128, 64), BF16),
             pltpu.VMEM((32, 64, 128), F32),
             sems(16),
         ],
@@ -1057,7 +1089,7 @@
         cost_estimate=cost(512 * 2 * 64 * 64 * 256, 17 * 2**20),
         name="weight_gradient",
     )(
-        in_vmem(coeffs),
+        in_vmem(turned),
         in_vmem(pairs),
     )
 

time: 89.8 us -> 93.1 us (1.037)
  local copies, waits for them, and re-layouts: 0.04 us -> 4.4 us
  waiting for transfers between devices: 11.7 us -> 8.69 us
  Pallas kernels: 49 us -> 50.9 us
    unnamed x12 -> x22, local copies, waits for them, and re-layouts: 0.04 us -> 4.4 us
    pallas_call x3, Pallas kernels: 18 us -> 21.9 us  [the longest x1 10.7 us: fast_body(): pl.pallas_call(weight_grad_kernel, out_shape=jax.ShapeDtypeStruct(spectra...]
    all_to_all x3, waiting for transfers between devices: 11.7 us -> 8.69 us  [exchange(): lax.all_to_all(block.reshape(devices, 64, 128), 'gx', 0, 0, tiled=True)]
    pallas_call x1, Pallas kernels: 8.17 us -> 6.9 us  [fast_body(): pl.pallas_call(functools.partial(mode_grad_kernel, forward_scale), out_sh...]
  transfers between devices with their start and end apart: 3 -> 3, of which waited for: 3 -> 2; matrix products, arithmetic and copies ran while one was open for 0% -> 0% of each run, Pallas kernels for 20% -> 24%
where the time goes in v4:
time: 93.1 us; the launch traced here: 92.5 us
  Pallas kernels  50.9 us (55%)
  starting transfers between devices  14.7 us (16%)
  blocking collectives  12.8 us (14%)
  waiting for transfers between devices  8.69 us (9%)
  local copies, waits for them, and re-layouts  4.4 us (5%)
  between operations  0.98 us (1%)
    all_to_all x3, starting transfers between devices, exchange(): lax.all_to_all(block.reshape(devices, 64, 128), 'gx', 0, 0, tiled=True)  14.7 us
    all_to_all x1, blocking collectives, exchange(): lax.all_to_all(block.reshape(devices, 64, 128), 'gx', 0, 0, tiled=True)  12.8 us
    pallas_call x1, Pallas kernels, fast_body(): pl.pallas_call(weight_grad_kernel, out_shape=jax.ShapeDtypeStruct(spectra...  10.7 us
    all_to_all x3, waiting for transfers between devices, exchange(): lax.all_to_all(block.reshape(devices, 64, 128), 'gx', 0, 0, tiled=True)  8.69 us
    pallas_call x1, Pallas kernels, fast_body(): pl.pallas_call(functools.partial(middle_kernel, inverse_scale), out_shape...  8.34 us
    pallas_call x1, Pallas kernels, fast_body(): pl.pallas_call(functools.partial(mode_grad_kernel, forward_scale), out_sh...  6.9 us
    pallas_call x1, Pallas kernels, fast_body(): pl.pallas_call(functools.partial(point_turn_kernel, weight_scale), out_sh...  6.19 us
    pallas_call x1, Pallas kernels, fast_body(): pl.pallas_call(functools.partial(mode_kernel, forward_scale), out_shape=[...  6.11 us
  transfers between devices with their start and end apart: 3, of which 2 were waited for; matrix products, arithmetic and copies ran while one was open for 0% of the time, Pallas kernels for 24%

profile of v4, /device:TPU:0, one launch (start us, length us, event | category | flops | bytes accessed | tf_op | source)
XLA Modules:
  0.0 92.5 jit_solution(13474222204897045845)
XLA Ops:
  0.6 0.0 copy-start.6
  0.6 3.8 %field_analysis.1 = bf16[1024,128]{1,0:T(8,128)(2,1)} custom-call(bf16[64,2,64,128]{3,2,1,0:T(8,128)(2,1)} %field_hbm.3, bf16[64,256]{1,0:T(8,128)(2,1)} %constant.17.clone.pair_hbm, bf16[128,256]{1,0:T(8,128)(2,1)} %constant.18.clone.across_hbm), custom_call_target="tpu_custom_call" | custom-call | flops 536870912 | bytes 2097152 | tf_op jit(solution)/shard_map/field_analysis/pallas_call | solution.py:947
  4.4 7.4 %all-to-all-start = ((bf16[16,64,128]{2,1,0:T(8,128)(2,1)}), bf16[16,64,128]{2,1,0:T(8,128)(2,1)S(1)}, u32[]{:S(2)}, u32[]{:S(2)}) async-start(bf16[16,64,128]{2,1,0:T(8,128)(2,1)} %bitcast), calls=%async_computation | async-start | bytes 524288 | tf_op jit(solution)/shard_map/all_to_all | solution.py:929
  11.8 0.0 copy-done.6
  11.8 0.0 copy-start.5
  11.8 0.0 copy-start.8
  11.8 0.0 copy-start.9
  11.8 5.1 %channel_map.1 = (bf16[64,2,64,128]{3,2,1,0:T(8,128)(2,1)}, bf16[12288,128]{1,0:T(8,128)(2,1)S(1)}) custom-call(bf16[64,64]{1,0:T(8,128)(2,1)S(1)} %copy-done.6, bf16[64,2,64,128]{3,2,1,0:T(8,128)(2,1)} %field_hbm.3, bf16[65536,128]{1,0:T(8,128)(2,1)} %bitcast.15), custom_call_target="tpu_custom_call" | custom-call | flops 2147483648 | bytes 4194304 | tf_op jit(solution)/shard_map/channel_map/pallas_call | solution.py:965
  16.9 4.9 %all-to-all-done = bf16[16,64,128]{2,1,0:T(8,128)(2,1)S(1)} async-done(((bf16[16,64,128]{2,1,0:T(8,128)(2,1)}), bf16[16,64,128]{2,1,0:T(8,128)(2,1)S(1)}, u32[]{:S(2)}, u32[]{:S(2)}) %all-to-all-start) | async-done | bytes 262176 | tf_op jit(solution)/shard_map/all_to_all | solution.py:929
  21.8 0.0 copy-done.5
  21.8 0.0 copy-done.8
  21.8 0.0 copy-start.10
  21.8 6.1 %mode_product.1 = (bf16[16,64,128]{2,1,0:T(8,128)(2,1)}, bf16[1024,128]{1,0:T(8,128)(2,1)S(1)}) custom-call(bf16[1024,128]{1,0:T(8,128)(2,1)S(1)} %bitcast.10, bf16[12288,128]{1,0:T(8,128)(2,1)S(1)} %get-tuple-element.26.head_ref, bf16[65536,128]{1,0:T(8,128)(2,1)} %bitcast.16, bf16[128,64]{1,0:T(8,128)(2,1)S(1)} %copy-done.8, bf16[64,64]{1,0:T(8,128)(2,1)S(1)} %copy-done.9, ...), custom_call_target="tpu_custom_call" | custom-call | flops 268435456 | bytes 17825792 | tf_op jit(solution)/shard_map/mode_product/pallas_call | solution.py:982
  28.0 12.8 %all_to_all.20 = bf16[16,64,128]{2,1,0:T(8,128)(2,1)S(1)} all-to-all(bf16[16,64,128]{2,1,0:T(8,128)(2,1)S(1)} %bitcast.14), channel_id=1, replica_groups=mesh['grp'=2,'gx'=16] {'gx'}, dimensions={0} | all-to-all | bytes 524288 | tf_op jit(solution)/shard_map/all_to_all | solution.py:929
  40.8 8.3 %gelu_and_gradient.1 = (bf16[64,2,64,128]{3,2,1,0:T(8,128)(2,1)}, bf16[64,2,64,128]{3,2,1,0:T(8,128)(2,1)}, bf16[1024,128]{1,0:T(8,128)(2,1)}) custom-call(bf16[1024,128]{1,0:T(8,128)(2,1)S(1)} %bitcast.12, f32[64]{0:T(128)S(1)} %copy-done.10, bf16[64,2,64,128]{3,2,1,0:T(8,128)(2,1)} %get-tuple-element.28.point_hbm, bf16[64,2,64,128]{3,2,1,0:T(8,128)(2,1)} %cot_hbm.1, ...), custom_call_target="tpu_custom_call" | custom-call | flops 1073741824 | bytes 8388608 | tf_op jit(solution)/shard_map/gelu_and_gradient/pallas_call | solution.py:1003
  49.1 3.5 %all-to-all-start.2 = ((bf16[16,64,128]{2,1,0:T(8,128)(2,1)}), bf16[16,64,128]{2,1,0:T(8,128)(2,1)S(1)}, u32[]{:S(2)}, u32[]{:S(2)}) async-start(bf16[16,64,128]{2,1,0:T(8,128)(2,1)} %bitcast.5), calls=%async_computation.2 | async-start | bytes 524288 | tf_op jit(solution)/shard_map/all_to_all | solution.py:929
  52.7 0.0 copy-start.7
  52.7 6.2 %channel_map_back.1 = (bf16[64,2,64,128]{3,2,1,0:T(8,128)(2,1)}, bf16[12288,128]{1,0:T(8,128)(2,1)S(1)}, bf16[16,128,64]{2,1,0:T(8,128)(2,1)}) custom-call(bf16[64,64]{1,0:T(8,128)(2,1)S(1)} %copy-done.6, bf16[64,2,64,128]{3,2,1,0:T(8,128)(2,1)} %get-tuple-element.31.field_hbm, bf16[65536,128]{1,0:T(8,128)(2,1)} %bitcast.17, ...), custom_call_target="tpu_custom_call" | custom-call | flops 2147483648 | bytes 4194304 | tf_op jit(solution)/shard_map/channel_map_back/pallas_call | solution.py:1039
  58.9 3.8 %all-to-all-done.2 = bf16[16,64,128]{2,1,0:T(8,128)(2,1)S(1)} async-done(((bf16[16,64,128]{2,1,0:T(8,128)(2,1)}), bf16[16,64,128]{2,1,0:T(8,128)(2,1)S(1)}, u32[]{:S(2)}, u32[]{:S(2)}) %all-to-all-start.2) | async-done | bytes 262176 | tf_op jit(solution)/shard_map/all_to_all | solution.py:929
  62.7 0.0 copy-done.7
  62.7 6.9 %mode_gradient.1 = (bf16[32,64,128]{2,1,0:T(8,128)(2,1)S(1)}, bf16[16,128,64]{2,1,0:T(8,128)(2,1)S(1)}, bf16[1024,128]{1,0:T(8,128)(2,1)S(1)}) custom-call(bf16[1024,128]{1,0:T(8,128)(2,1)S(1)} %bitcast.9, bf16[12288,128]{1,0:T(8,128)(2,1)S(1)} %get-tuple-element.37.head_ref, bf16[65536,128]{1,0:T(8,128)(2,1)} %bitcast.18, bf16[128,64]{1,0:T(8,128)(2,1)S(1)} %copy-done.7, ...), custom_call_target="tpu_custom_call" | custom-call | flops 268435456 | bytes 17825792 | tf_op jit(solution)/shard_map/mode_gradient/pallas_call | solution.py:1054
  69.6 0.0 copy-start
  69.6 0.8 copy-done
  70.4 0.8 copy-done.2
  71.2 0.7 copy-done.4
  71.9 3.8 %all-to-all-start.3 = ((bf16[16,64,128]{2,1,0:T(8,128)(2,1)}), bf16[16,64,128]{2,1,0:T(8,128)(2,1)S(1)}, u32[]{:S(2)}, u32[]{:S(2)}) async-start(bf16[16,64,128]{2,1,0:T(8,128)(2,1)} %bitcast.13), calls=%async_computation.3 | async-start | bytes 524288 | tf_op jit(solution)/shard_map/all_to_all | solution.py:929
  75.7 0.0 copy-start.1
  75.7 1.0 %copy-done.1 = bf16[32,64,128]{2,1,0:T(8,128)(2,1)S(1)} copy-done((bf16[32,64,128]{2,1,0:T(8,128)(2,1)S(1)}, bf16[32,64,128]{2,1,0:T(8,128)(2,1)}, u32[]{:S(2)}) %copy-start.1) | copy-done | bytes 524312
  76.7 1.0 %copy-done.3 = bf16[16,128,64]{2,1,0:T(8,128)(2,1)S(1)} copy-done((bf16[16,128,64]{2,1,0:T(8,128)(2,1)S(1)}, bf16[16,128,64]{2,1,0:T(8,128)(2,1)}, u32[]{:S(2)}) %copy-start.3) | copy-done | bytes 262168
  77.7 10.7 %weight_gradient.1 = bf16[1024,64,128]{2,1,0:T(8,128)(2,1)} custom-call(bf16[16,128,64]{2,1,0:T(8,128)(2,1)S(1)} %copy-done.3, bf16[32,64,128]{2,1,0:T(8,128)(2,1)S(1)} %copy-done.1), custom_call_target="tpu_custom_call" | custom-call | flops 1073741824 | bytes 17825792 | tf_op jit(solution)/shard_map/weight_gradient/pallas_call | solution.py:1077
  88.4 0.0 all-to-all-done.3
  88.4 3.9 %field_gradient.1 = bf16[64,2,64,128]{3,2,1,0:T(8,128)(2,1)} custom-call(bf16[1024,128]{1,0:T(8,128)(2,1)S(1)} %bitcast.11, bf16[64,2,64,128]{3,2,1,0:T(8,128)(2,1)} %get-tuple-element.40.point_hbm, bf16[256,1024]{1,0:T(8,128)(2,1)} %constant.16.clone.depth_hbm, bf16[256,128]{1,0:T(8,128)(2,1)} %constant.19.clone.back_hbm), custom_call_target="tpu_custom_call" | custom-call | flops 536870912 | bytes 4194304 | tf_op jit(solution)/shard_map/field_gradient/pallas_call | solution.py:1096
  (5 shorter events, 0.0 us)
Async XLA Ops:
  0.6 11.2 %copy-start.6 = (bf16[64,64]{1,0:T(8,128)(2,1)S(1)}, bf16[64,64]{1,0:T(8,128)(2,1)}, u32[]{:S(2)}) copy-start(bf16[64,64]{1,0:T(8,128)(2,1)} %weight_ref.3) | copy-start | bytes 24580
  4.4 17.4 %all-to-all-start = ((bf16[16,64,128]{2,1,0:T(8,128)(2,1)}), bf16[16,64,128]{2,1,0:T(8,128)(2,1)S(1)}, u32[]{:S(2)}, u32[]{:S(2)}) async-start(bf16[16,64,128]{2,1,0:T(8,128)(2,1)} %bitcast), calls=%async_computation | async-start | bytes 524288 | tf_op jit(solution)/shard_map/all_to_all | solution.py:929
  11.8 10.0 %copy-start.5 = (bf16[64,64]{1,0:T(8,128)(2,1)S(1)}, bf16[64,64]{1,0:T(8,128)(2,1)}, u32[]{:S(2)}) copy-start(bf16[64,64]{1,0:T(8,128)(2,1)} %constant.23.clone.back_ref) | copy-start | bytes 24580
  11.8 10.0 %copy-start.8 = (bf16[128,64]{1,0:T(8,128)(2,1)S(1)}, bf16[128,64]{1,0:T(8,128)(2,1)}, u32[]{:S(2)}) copy-start(bf16[128,64]{1,0:T(8,128)(2,1)} %constant.21.clone.both_ref) | copy-start | bytes 49156
  11.8 10.0 %copy-start.9 = (bf16[64,64]{1,0:T(8,128)(2,1)S(1)}, bf16[64,64]{1,0:T(8,128)(2,1)}, u32[]{:S(2)}) copy-start(bf16[64,64]{1,0:T(8,128)(2,1)} %constant.20.clone.plain_ref) | copy-start | bytes 24580
  21.8 19.0 %copy-start.10 = (f32[64]{0:T(128)S(1)}, f32[64]{0:T(128)}, u32[]{:S(2)}) copy-start(f32[64]{0:T(128)} %bias_ref.1) | copy-start | bytes 772
  49.1 13.6 %all-to-all-start.2 = ((bf16[16,64,128]{2,1,0:T(8,128)(2,1)}), bf16[16,64,128]{2,1,0:T(8,128)(2,1)S(1)}, u32[]{:S(2)}, u32[]{:S(2)}) async-start(bf16[16,64,128]{2,1,0:T(8,128)(2,1)} %bitcast.5), calls=%async_computation.2 | async-start | bytes 524288 | tf_op jit(solution)/shard_map/all_to_all | solution.py:929
  52.7 10.0 %copy-start.7 = (bf16[128,64]{1,0:T(8,128)(2,1)S(1)}, bf16[128,64]{1,0:T(8,128)(2,1)}, u32[]{:S(2)}) copy-start(bf16[128,64]{1,0:T(8,128)(2,1)} %constant.22.clone.straight_ref) | copy-start | bytes 49156
  69.6 0.8 copy-start
  70.4 0.8 copy-start.2
  71.2 0.7 copy-start.4
  71.9 16.5 %all-to-all-start.3 = ((bf16[16,64,128]{2,1,0:T(8,128)(2,1)}), bf16[16,64,128]{2,1,0:T(8,128)(2,1)S(1)}, u32[]{:S(2)}, u32[]{:S(2)}) async-start(bf16[16,64,128]{2,1,0:T(8,128)(2,1)} %bitcast.13), calls=%async_computation.3 | async-start | bytes 524288 | tf_op jit(solution)/shard_map/all_to_all | solution.py:929
  75.7 1.0 %copy-start.1 = (bf16[32,64,128]{2,1,0:T(8,128)(2,1)S(1)}, bf16[32,64,128]{2,1,0:T(8,128)(2,1)}, u32[]{:S(2)}) copy-start(bf16[32,64,128]{2,1,0:T(8,128)(2,1)} %copy-done) | copy-start | bytes 1572868
  76.7 1.0 %copy-start.3 = (bf16[16,128,64]{2,1,0:T(8,128)(2,1)S(1)}, bf16[16,128,64]{2,1,0:T(8,128)(2,1)}, u32[]{:S(2)}) copy-start(bf16[16,128,64]{2,1,0:T(8,128)(2,1)} %copy-done.2) | copy-start | bytes 786436
